TPU v7x, 256 devices: a whole 4x4x8 slice. The times are simulated.
256 devices in a mesh: grp: 4 (over x_lo, core), col: 64 (over z, x_hi, y).
Axes of the slice: x: 4 (x_hi: 2, x_lo: 2; x = x_hi * 2 + x_lo), y: 4, z: 8, core: 2. Of those that a mesh axis runs over, the one named last changes fastest.
Arguments:
- embeddings: float32 [32768, 512], P(('grp', 'col'))
- cluster_sizes: int32 [4], P('grp'), may hold values from 2048 to 8192, as said below
Outputs:
- nearest: float32 [32768], P(('grp', 'col'))
Inputs may be any that keep to these rules, and one draw needn't show every extreme that they name: `cluster_sizes`: every cluster has between a quarter of 8192 and 8192 live rows; at least one cluster is full.
All inputs are finite; a program needn't handle non-finite values.
Results may differ from a plain program's by a relative error of at most 0.00039.
Values may be sent and summed in bfloat16 or wider, within the bound.
No kernel may reach another device: no remote copies, remote signals or barrier semaphores. Data moves between devices by JAX's collectives and lax.ppermute only.
A program may use at most 64 MiB of HBM per device.

v0:
```python
import jax
import jax.numpy as jnp
from jax import lax
from jax.experimental import pallas as pl
from jax.experimental.pallas import tpu as pltpu
from jax.sharding import Mesh, PartitionSpec as P

AXES = ("xl", "core", "z", "xh", "y")
SIZES = (2, 2, 8, 2, 4)
GRID = (8, 2, 4)
BLOCKS = 64
EMPTY = -2.0
FIRST = ((0, 0, 0), (3, 0, 0), (0, 0, 2), (7, 1, 1))
SECOND = ((0, 0, 0), (0, 0, 1), (1, 0, 0))


def minus(a, b):
    return tuple((x - y) % n for x, y, n in zip(a, b, GRID))


def tiles():
    steps = [
        tuple((x + y) % n for x, y, n in zip(f, s, GRID)) for s in SECOND for f in FIRST
    ]
    missing = {
        (z, x, y) for z in range(GRID[0]) for x in range(GRID[1]) for y in range(GRID[2])
    }
    missing.discard((0, 0, 0))
    chosen = {0: [0]}
    while missing:
        best = []
        for i, a in enumerate(steps):
            found, seen = [], set()
            for j, b in enumerate(steps):
                d = minus(b, a)
                if d in missing and d not in seen:
                    seen |= {d, minus(a, b)}
                    found.append(j)
            if len(found) > len(best):
                row, best = i, found
        for j in best:
            missing -= {minus(steps[j], steps[row]), minus(steps[row], steps[j])}
        chosen[row] = chosen.get(row, []) + best
    return steps, chosen


STEPS, TILES = tiles()


def send(array, step, sign):
    size = BLOCKS
    pairs = []
    for core in range(2):
        way = sign if core == 0 else -sign
        for i in range(size):
            at = (i // 8, i // 4 % 2, i % 4)
            z, x, y = ((a + way * s) % n for a, s, n in zip(at, step, GRID))
            pairs.append((core * size + i, core * size + z * 8 + x * 4 + y))
    return lax.ppermute(array, ("core", "z", "xh", "y"), pairs)


def head_kernel(own_ref, sums_ref):
    sums_ref[...] = jnp.broadcast_to(
        jnp.sum(own_ref[...], axis=0, keepdims=True)[None], sums_ref.shape
    )


def middle_kernel(sums_ref, *refs):
    out_ref, pack_ref = refs[-2:]
    out_ref[...] = jnp.broadcast_to(
        jnp.sum(sums_ref[...], axis=0, keepdims=True), out_ref.shape
    )
    for k, ref in enumerate(refs[:-2]):
        pack_ref[k] = ref[...]


def unit(rows, centre):
    shifted = rows - centre
    scale = lax.rsqrt(jnp.sum(shifted * shifted, axis=1, keepdims=True) + 1e-06)
    return (shifted * scale).astype(jnp.bfloat16)


def best_kernel(live_ref, sums_ref, *refs):
    n = len(SECOND)
    held, found, units = refs[:n], refs[n : 2 * n], refs[2 * n]
    rows = held[0].shape[1]
    per = len(FIRST)
    centre = jnp.sum(sums_ref[...], axis=0) / (rows * 4 * BLOCKS)
    live = live_ref[0]
    core = lax.axis_index("core")
    at = [lax.axis_index(a) for a in ("z", "xh", "y")]
    lane = lax.broadcasted_iota(jnp.int32, (1, rows), 1)
    sublane = lax.broadcasted_iota(jnp.int32, (rows, 1), 0)
    starts = []
    for k, step in enumerate(STEPS):
        units[k] = unit(held[k // per][k % per], centre)
        z, x, y = (
            lax.rem(a + jnp.where(core == 0, m - s, s), m)
            for a, s, m in zip(at, step, GRID)
        )
        starts.append((z * 8 + x * 4 + y) * rows)
    best = [None] * len(STEPS)

    def merge(k, line):
        best[k] = line if best[k] is None else jnp.maximum(best[k], line)

    for i, columns in TILES.items():
        row_ids = starts[i] + sublane
        folded = None
        for j in columns:
            scores = lax.dot_general(
                units[i],
                units[j],
                (((1,), (1,)), ((), ())),
                preferred_element_type=jnp.float32,
            )
            col_ids = starts[j] + lane
            valid = (row_ids < live) & (col_ids < live)
            if i == j:
                valid = valid & (row_ids != col_ids)
            scores = jnp.where(valid, scores, EMPTY)
            merge(j, jnp.max(scores, axis=0, keepdims=True))
            if i != j:
                folded = scores if folded is None else jnp.maximum(folded, scores)
        if folded is not None:
            merge(i, jnp.max(folded.T, axis=0, keepdims=True))
    for k in range(len(STEPS)):
        line = jnp.full((1, rows), EMPTY, jnp.float32) if best[k] is None else best[k]
        found[k // per][k % per] = line


def merge_kernel(*refs):
    n = len(SECOND)
    best = refs[0][...]
    for ref in refs[1:n]:
        best = jnp.maximum(best, ref[...])
    for k, ref in enumerate(refs[n:]):
        ref[...] = best[k]


def shards(embeddings, cluster_sizes):
    rows, width = embeddings.shape
    vmem = pl.BlockSpec(memory_space=pltpu.VMEM)
    small = pltpu.CompilerParams(vmem_limit_bytes=4 * 1024 * 1024)
    first, second = len(FIRST), len(SECOND)
    arrived = [send(embeddings, step, 1) for step in FIRST[1:]]
    sums = pl.pallas_call(
        head_kernel,
        out_shape=jax.ShapeDtypeStruct((GRID[0], 1, width), jnp.float32),
        in_specs=[vmem],
        out_specs=vmem,
        compiler_params=small,
    )(embeddings)
    sums = lax.all_to_all(sums, "z", 0, 0)
    sums, held = pl.pallas_call(
        middle_kernel,
        out_shape=(
            jax.ShapeDtypeStruct((32, 1, width), jnp.float32),
            jax.ShapeDtypeStruct((first, rows, width), jnp.float32),
        ),
        in_specs=[vmem] * (first + 1),
        out_specs=(vmem,) * 2,
        compiler_params=small,
    )(sums, embeddings, *arrived)
    sums = lax.all_to_all(sums, ("xl", "core", "xh", "y"), 0, 0)
    held = [held] + [send(held, step, 1) for step in SECOND[1:]]
    found = pl.pallas_call(
        best_kernel,
        out_shape=(jax.ShapeDtypeStruct((first, 1, rows), jnp.float32),) * second,
        in_specs=[pl.BlockSpec(memory_space=pltpu.SMEM)] + [vmem] * (second + 1),
        out_specs=(vmem,) * second,
        scratch_shapes=[pltpu.VMEM((first * second, rows, width), jnp.bfloat16)],
        compiler_params=pltpu.CompilerParams(vmem_limit_bytes=20 * 1024 * 1024),
    )(cluster_sizes, sums, *held)
    back = [send(f, step, -1) for f, step in zip(found[1:], SECOND[1:])]
    lines = pl.pallas_call(
        merge_kernel,
        out_shape=(jax.ShapeDtypeStruct((1, rows), jnp.float32),) * first,
        in_specs=[vmem] * second,
        out_specs=(vmem,) * first,
        compiler_params=small,
    )(found[0], *back)
    best = lines[0]
    for line, step in zip(lines[1:], FIRST[1:]):
        best = jnp.maximum(best, send(line, step, -1))
    block = lax.axis_index("z") * 8 + lax.axis_index("xh") * 4 + lax.axis_index("y")
    row_ids = block * rows + jnp.arange(rows, dtype=jnp.int32)
    return jnp.where(row_ids < cluster_sizes[0], best[0], jnp.float32(0.0))


def solution(mesh):
    fine = Mesh(mesh.devices.reshape(SIZES), AXES)
    return jax.shard_map(
        shards,
        mesh=fine,
        in_specs=(P(AXES, None), P(("xl", "core"))),
        out_specs=P(AXES),
        check_vma=False,
    )
```

profile of v0, /device:TPU:1, one launch (start us, length us, event | category | flops | bytes accessed | tf_op | source)
XLA Modules:
  0.0 60.7 jit_solution(8443615551378178289)
XLA Ops:
  0.0 7.3 %collective-permute-start = (f32[128,512]{1,0:T(8,128)}, f32[128,512]{1,0:T(8,128)S(1)}, u32[]{:S(2)}, u32[]{:S(2)}) collective-permute-start(f32[128,512]{1,0:T(8,128)} %refs_0_.1), channel_id=1, source_target_pairs={{0,24},{1,25},{2,26},{3,27},{4,28},{5,29},{6,30},{7,31},{8,32},{9,... | collective-permute-start | bytes 786440 | tf_op jit(solution)/shard_map/ppermute | solution.py:59
  7.3 2.9 %collective-permute-start.1 = (f32[128,512]{1,0:T(8,128)}, f32[128,512]{1,0:T(8,128)S(1)}, u32[]{:S(2)}, u32[]{:S(2)}) collective-permute-start(f32[128,512]{1,0:T(8,128)} %refs_0_.1), channel_id=1, source_target_pairs={{0,2},{1,3},{2,0},{3,1},{4,6},{5,7},{6,4},{7,5},{8,10},{9,11},{10,... | collective-permute-start | bytes 786440 | tf_op jit(solution)/shard_map/ppermute | solution.py:59
  10.2 3.7 %collective-permute-start.2 = (f32[128,512]{1,0:T(8,128)}, f32[128,512]{1,0:T(8,128)S(1)}, u32[]{:S(2)}, u32[]{:S(2)}) collective-permute-start(f32[128,512]{1,0:T(8,128)} %refs_0_.1), channel_id=1, source_target_pairs={{0,61},{1,62},{2,63},{3,60},{4,57},{5,58},{6,59},{7,56},{8,5},{9,6... | collective-permute-start | bytes 786440 | tf_op jit(solution)/shard_map/ppermute | solution.py:59
  13.9 0.0 copy-start
  13.9 1.0 %copy-done = f32[128,512]{1,0:T(8,128)S(1)} copy-done((f32[128,512]{1,0:T(8,128)S(1)}, f32[128,512]{1,0:T(8,128)}, u32[]{:S(2)}) %copy-start) | copy-done | bytes 262168
  14.9 9.6 %all_to_all.10.sums_ref = f32[8,1,512]{2,1,0:T(1,128)S(1)} all-to-all(f32[8,1,512]{2,1,0:T(1,128)S(1)} %shard_map.28), channel_id=1, replica_groups=mesh['xl'=2,'core'=2,'z'=8,'xh'=2,'y'=4] {'z'}, dimensions={0} | all-to-all | bytes 32768 | tf_op jit(solution)/shard_map/all_to_all | solution.py:154
  24.6 0.0 collective-permute-done.refs_1_
  24.6 0.0 collective-permute-done.1.refs_2_
  24.6 0.0 collective-permute-done.2.refs_3_
  24.6 0.7 %shard_map.29 = (f32[32,1,512]{2,1,0:T(1,128)}, f32[4,128,512]{2,1,0:T(8,128)S(1)}) custom-call(f32[8,1,512]{2,1,0:T(1,128)S(1)} %all_to_all.10.sums_ref, f32[128,512]{1,0:T(8,128)S(1)} %copy-done, f32[128,512]{1,0:T(8,128)S(1)} %collective-permute-done.refs_1_, f32[128,512]{1,0:T(8,128)S(1)} %collective-permute-done.1.refs_2_, ...), custom_call_target="tpu_custom_call" | custom-call | tf_op jit(solution)/shard_map/pallas_call | solution.py:155
  25.3 0.5 collective-permute-start.3
  25.8 0.5 collective-permute-start.4
  26.3 9.6 %all-to-all-start.1 = ((f32[32,1,512]{2,1,0:T(1,128)}), f32[32,1,512]{2,1,0:T(1,128)S(1)}, u32[]{:S(2)}, u32[]{:S(2)}) async-start(f32[32,1,512]{2,1,0:T(1,128)} %get-tuple-element.14), calls=%async_computation.1 | async-start | bytes 131072 | tf_op jit(solution)/shard_map/all_to_all | solution.py:165
  36.5 9.4 %all-to-all-done.1.sums_ref = f32[32,1,512]{2,1,0:T(1,128)S(1)} async-done(((f32[32,1,512]{2,1,0:T(1,128)}), f32[32,1,512]{2,1,0:T(1,128)S(1)}, u32[]{:S(2)}, u32[]{:S(2)}) %all-to-all-start.1) | async-done | bytes 65568 | tf_op jit(solution)/shard_map/all_to_all | solution.py:165
  45.9 0.0 collective-permute-done.3.refs_1_
  45.9 0.0 collective-permute-done.4.refs_2_
  45.9 1.9 %shard_map.30 = (f32[4,1,128]{2,1,0:T(1,128)S(1)}, f32[4,1,128]{2,1,0:T(1,128)S(1)}, f32[4,1,128]{2,1,0:T(1,128)S(1)}) custom-call(s32[1]{0:T(128)} %copy.3.live_ref, f32[32,1,512]{2,1,0:T(1,128)S(1)} %all-to-all-done.1.sums_ref, f32[4,128,512]{2,1,0:T(8,128)S(1)} %get-tuple-element.15.refs_0_, f32[4,128,512]{2,1,0:T(8,128)S(1)} %collective-permute-done.3.refs_1_, ...), custom_call_target="tpu_custom_call" | custom-call | tf_op jit(solution)/shard_map/pallas_call | solution.py:167
  47.8 0.1 collective-permute-start.5
  47.9 0.5 collective-permute-start.6
  48.4 3.2 %collective-permute-done.5.refs_1_ = f32[4,1,128]{2,1,0:T(1,128)S(1)} collective-permute-done((f32[4,1,128]{2,1,0:T(1,128)S(1)}, f32[4,1,128]{2,1,0:T(1,128)S(1)}, u32[]{:S(2)}, u32[]{:S(2)}) %collective-permute-start.5) | collective-permute-done | bytes 2080 | tf_op jit(solution)/shard_map/ppermute | solution.py:59
  51.5 0.1 collective-permute-done.6.refs_2_
  51.6 0.0 collective-permute-start.9
  51.7 3.2 %collective-permute-start.8 = (f32[1,128]{1,0:T(1,128)S(1)}, f32[1,128]{1,0:T(1,128)S(1)}, u32[]{:S(2)}, u32[]{:S(2)}) collective-permute-start(f32[1,128]{1,0:T(1,128)S(1)} %get-tuple-element.21), channel_id=1, source_target_pairs={{0,2},{1,3},{2,0},{3,1},{4,6},{5,7},{6,4},{7,5},{8,10},{9,11},{10,... | collective-permute-start | bytes 1544 | tf_op jit(solution)/shard_map/ppermute | solution.py:59
  54.8 0.8 %collective-permute-start.7 = (f32[1,128]{1,0:T(1,128)S(1)}, f32[1,128]{1,0:T(1,128)S(1)}, u32[]{:S(2)}, u32[]{:S(2)}) collective-permute-start(f32[1,128]{1,0:T(1,128)S(1)} %get-tuple-element.20), channel_id=1, source_target_pairs={{0,40},{1,41},{2,42},{3,43},{4,44},{5,45},{6,46},{7,47},{8,48},{9,... | collective-permute-start | bytes 1544 | tf_op jit(solution)/shard_map/ppermute | solution.py:59
  55.6 2.9 %collective-permute-done.9 = f32[1,128]{1,0:T(1,128)S(1)} collective-permute-done((f32[1,128]{1,0:T(1,128)S(1)}, f32[1,128]{1,0:T(1,128)S(1)}, u32[]{:S(2)}, u32[]{:S(2)}) %collective-permute-start.9) | collective-permute-done | bytes 544 | tf_op jit(solution)/shard_map/ppermute | solution.py:59
  58.5 0.0 collective-permute-done.8
  58.6 1.7 %collective-permute-done.7 = f32[1,128]{1,0:T(1,128)S(1)} collective-permute-done((f32[1,128]{1,0:T(1,128)S(1)}, f32[1,128]{1,0:T(1,128)S(1)}, u32[]{:S(2)}, u32[]{:S(2)}) %collective-permute-start.7) | collective-permute-done | bytes 544 | tf_op jit(solution)/shard_map/ppermute | solution.py:59
  60.2 0.5 compare_select_fusion
  (2 shorter events, 0.0 us)
Async XLA Ops:
  0.0 24.6 %collective-permute-start = (f32[128,512]{1,0:T(8,128)}, f32[128,512]{1,0:T(8,128)S(1)}, u32[]{:S(2)}, u32[]{:S(2)}) collective-permute-start(f32[128,512]{1,0:T(8,128)} %refs_0_.1), channel_id=1, source_target_pairs={{0,24},{1,25},{2,26},{3,27},{4,28},{5,29},{6,30},{7,31},{8,32},{9,... | collective-permute-start | bytes 786440 | tf_op jit(solution)/shard_map/ppermute | solution.py:59
  7.3 17.3 %collective-permute-start.1 = (f32[128,512]{1,0:T(8,128)}, f32[128,512]{1,0:T(8,128)S(1)}, u32[]{:S(2)}, u32[]{:S(2)}) collective-permute-start(f32[128,512]{1,0:T(8,128)} %refs_0_.1), channel_id=1, source_target_pairs={{0,2},{1,3},{2,0},{3,1},{4,6},{5,7},{6,4},{7,5},{8,10},{9,11},{10,... | collective-permute-start | bytes 786440 | tf_op jit(solution)/shard_map/ppermute | solution.py:59
  10.2 14.4 %collective-permute-start.2 = (f32[128,512]{1,0:T(8,128)}, f32[128,512]{1,0:T(8,128)S(1)}, u32[]{:S(2)}, u32[]{:S(2)}) collective-permute-start(f32[128,512]{1,0:T(8,128)} %refs_0_.1), channel_id=1, source_target_pairs={{0,61},{1,62},{2,63},{3,60},{4,57},{5,58},{6,59},{7,56},{8,5},{9,6... | collective-permute-start | bytes 786440 | tf_op jit(solution)/shard_map/ppermute | solution.py:59
  13.9 1.0 %copy-start = (f32[128,512]{1,0:T(8,128)S(1)}, f32[128,512]{1,0:T(8,128)}, u32[]{:S(2)}) copy-start(f32[128,512]{1,0:T(8,128)} %refs_0_.1) | copy-start | bytes 786436
  25.3 20.7 %collective-permute-start.3 = (f32[4,128,512]{2,1,0:T(8,128)S(1)}, f32[4,128,512]{2,1,0:T(8,128)S(1)}, u32[]{:S(2)}, u32[]{:S(2)}) collective-permute-start(f32[4,128,512]{2,1,0:T(8,128)S(1)} %get-tuple-element.15.refs_0_), channel_id=1, source_target_pairs={{0,1},{1,2},{2,3},{3,0},{4,5},{5,6},{6,7},{7,4},{8,9},{9,10},{10,1... | collective-permute-start | bytes 3145736 | tf_op jit(solution)/shard_map/ppermute | solution.py:59
  25.8 20.2 %collective-permute-start.4 = (f32[4,128,512]{2,1,0:T(8,128)S(1)}, f32[4,128,512]{2,1,0:T(8,128)S(1)}, u32[]{:S(2)}, u32[]{:S(2)}) collective-permute-start(f32[4,128,512]{2,1,0:T(8,128)S(1)} %get-tuple-element.15.refs_0_), channel_id=1, source_target_pairs={{0,8},{1,9},{2,10},{3,11},{4,12},{5,13},{6,14},{7,15},{8,16},{9,17... | collective-permute-start | bytes 3145736 | tf_op jit(solution)/shard_map/ppermute | solution.py:59
  26.3 19.6 %all-to-all-start.1 = ((f32[32,1,512]{2,1,0:T(1,128)}), f32[32,1,512]{2,1,0:T(1,128)S(1)}, u32[]{:S(2)}, u32[]{:S(2)}) async-start(f32[32,1,512]{2,1,0:T(1,128)} %get-tuple-element.14), calls=%async_computation.1 | async-start | bytes 131072 | tf_op jit(solution)/shard_map/all_to_all | solution.py:165
  47.8 3.7 %collective-permute-start.5 = (f32[4,1,128]{2,1,0:T(1,128)S(1)}, f32[4,1,128]{2,1,0:T(1,128)S(1)}, u32[]{:S(2)}, u32[]{:S(2)}) collective-permute-start(f32[4,1,128]{2,1,0:T(1,128)S(1)} %get-tuple-element.17), channel_id=1, source_target_pairs={{0,3},{1,0},{2,1},{3,2},{4,7},{5,4},{6,5},{7,6},{8,11},{9,8},{10,9... | collective-permute-start | bytes 6152 | tf_op jit(solution)/shard_map/ppermute | solution.py:59
  47.9 3.7 %collective-permute-start.6 = (f32[4,1,128]{2,1,0:T(1,128)S(1)}, f32[4,1,128]{2,1,0:T(1,128)S(1)}, u32[]{:S(2)}, u32[]{:S(2)}) collective-permute-start(f32[4,1,128]{2,1,0:T(1,128)S(1)} %get-tuple-element.18), channel_id=1, source_target_pairs={{0,56},{1,57},{2,58},{3,59},{4,60},{5,61},{6,62},{7,63},{8,0},{9,1... | collective-permute-start | bytes 6152 | tf_op jit(solution)/shard_map/ppermute | solution.py:59
  51.6 6.9 %collective-permute-start.9 = (f32[1,128]{1,0:T(1,128)S(1)}, f32[1,128]{1,0:T(1,128)S(1)}, u32[]{:S(2)}, u32[]{:S(2)}) collective-permute-start(f32[1,128]{1,0:T(1,128)S(1)} %get-tuple-element.22), channel_id=1, source_target_pairs={{0,15},{1,12},{2,13},{3,14},{4,11},{5,8},{6,9},{7,10},{8,23},{9,20... | collective-permute-start | bytes 1544 | tf_op jit(solution)/shard_map/ppermute | solution.py:59
  51.7 6.9 %collective-permute-start.8 = (f32[1,128]{1,0:T(1,128)S(1)}, f32[1,128]{1,0:T(1,128)S(1)}, u32[]{:S(2)}, u32[]{:S(2)}) collective-permute-start(f32[1,128]{1,0:T(1,128)S(1)} %get-tuple-element.21), channel_id=1, source_target_pairs={{0,2},{1,3},{2,0},{3,1},{4,6},{5,7},{6,4},{7,5},{8,10},{9,11},{10,... | collective-permute-start | bytes 1544 | tf_op jit(solution)/shard_map/ppermute | solution.py:59
  54.8 5.4 %collective-permute-start.7 = (f32[1,128]{1,0:T(1,128)S(1)}, f32[1,128]{1,0:T(1,128)S(1)}, u32[]{:S(2)}, u32[]{:S(2)}) collective-permute-start(f32[1,128]{1,0:T(1,128)S(1)} %get-tuple-element.20), channel_id=1, source_target_pairs={{0,40},{1,41},{2,42},{3,43},{4,44},{5,45},{6,46},{7,47},{8,48},{9,... | collective-permute-start | bytes 1544 | tf_op jit(solution)/shard_map/ppermute | solution.py:59
where the time goes:
time: 60.9 us; the launch traced here: 60.7 us
  starting transfers between devices  29 us (48%)
  waiting for transfers between devices  17.3 us (28%)
  blocking collectives  9.64 us (16%)
  Pallas kernels  2.61 us (4%)
  local copies, waits for them, and re-layouts  0.98 us (2%)
  between operations  0.7 us (1%)
    ppermute x10, starting transfers between devices, send(): return lax.ppermute(array, ('core', 'z', 'xh', 'y'), pairs)  19.4 us
    all_to_all x1, blocking collectives, shards(): sums = lax.all_to_all(sums, 'z', 0, 0)  9.64 us
    all_to_all x1, starting transfers between devices, shards(): sums = lax.all_to_all(sums, ('xl', 'core', 'xh', 'y'), 0, 0)  9.6 us
    all_to_all x1, waiting for transfers between devices, shards(): sums = lax.all_to_all(sums, ('xl', 'core', 'xh', 'y'), 0, 0)  9.38 us
    ppermute x10, waiting for transfers between devices, send(): return lax.ppermute(array, ('core', 'z', 'xh', 'y'), pairs)  7.88 us
    pallas_call x1, Pallas kernels, shards(): pl.pallas_call(best_kernel, out_shape=(jax.ShapeDtypeStruct((first, 1, ro...  1.87 us
  transfers between devices with their start and end apart: 11, of which 5 were waited for; matrix products, arithmetic and copies ran while one was open for 0% of the time, Pallas kernels for 0%

commit v1 on v0

--- a/solution.py
+++ b/solution.py
@@ -10,7 +10,7 @@
 GRID = (8, 2, 4)
 BLOCKS = 64
 EMPTY = -2.0
-FIRST = ((0, 0, 0), (3, 0, 0), (0, 0, 2), (7, 1, 1))
+FIRST = ((0, 0, 0), (7, 1, 0), (3, 0, 1), (0, 0, 2))
 SECOND = ((0, 0, 0), (0, 0, 1), (1, 0, 0))
 
 
@@ -146,23 +146,23 @@
     arrived = [send(embeddings, step, 1) for step in FIRST[1:]]
     sums = pl.pallas_call(
         head_kernel,
-        out_shape=jax.ShapeDtypeStruct((GRID[0], 1, width), jnp.float32),
+        out_shape=jax.ShapeDtypeStruct((16, 1, width), jnp.float32),
         in_specs=[vmem],
         out_specs=vmem,
         compiler_params=small,
     )(embeddings)
-    sums = lax.all_to_all(sums, "z", 0, 0)
+    sums = lax.all_to_all(sums, ("core", "z"), 0, 0)
     sums, held = pl.pallas_call(
         middle_kernel,
         out_shape=(
-            jax.ShapeDtypeStruct((32, 1, width), jnp.float32),
+            jax.ShapeDtypeStruct((16, 1, width), jnp.float32),
             jax.ShapeDtypeStruct((first, rows, width), jnp.float32),
         ),
         in_specs=[vmem] * (first + 1),
         out_specs=(vmem,) * 2,
         compiler_params=small,
     )(sums, embeddings, *arrived)
-    sums = lax.all_to_all(sums, ("xl", "core", "xh", "y"), 0, 0)
+    sums = lax.all_to_all(sums, ("xl", "xh", "y"), 0, 0)
     held = [held] + [send(held, step, 1) for step in SECOND[1:]]
     found = pl.pallas_call(
         best_kernel,
@@ -181,8 +181,8 @@
         compiler_params=small,
     )(found[0], *back)
     best = lines[0]
-    for line, step in zip(lines[1:], FIRST[1:]):
-        best = jnp.maximum(best, send(line, step, -1))
+    for k in (2, 3, 1):
+        best = jnp.maximum(best, send(lines[k], FIRST[k], -1))
     block = lax.axis_index("z") * 8 + lax.axis_index("xh") * 4 + lax.axis_index("y")
     row_ids = block * rows + jnp.arange(rows, dtype=jnp.int32)
     return jnp.where(row_ids < cluster_sizes[0], best[0], jnp.float32(0.0))

time: 60.9 us -> 60.3 us (level)
  starting transfers between devices: 29 us -> 23 us
  blocking collectives: 9.64 us -> 13.6 us
  waiting for transfers between devices: 17.3 us -> 18.7 us
    all_to_all x1, starting transfers between devices: 9.6 us -> 3.48 us  [shards(): sums = lax.all_to_all(sums, ('xl', 'xh', 'y'), 0, 0)]
    all_to_all x1, blocking collectives: 9.64 us -> 13.6 us  [shards(): sums = lax.all_to_all(sums, ('core', 'z'), 0, 0)]
    ppermute x10, waiting for transfers between devices: 7.88 us -> 10.4 us  [send(): return lax.ppermute(array, ('core', 'z', 'xh', 'y'), pairs)]
    all_to_all x1, waiting for transfers between devices: 9.38 us -> 8.34 us  [shards(): sums = lax.all_to_all(sums, ('xl', 'xh', 'y'), 0, 0)]
  transfers between devices with their start and end apart: 11 -> 11, of which waited for: 5 -> 7; matrix products, arithmetic and copies ran while one was open for 0% -> 0% of each run, Pallas kernels for 0% -> 0%
where the time goes in v1:
time: 60.3 us; the launch traced here: 60.1 us
  starting transfers between devices  23 us (38%)
  waiting for transfers between devices  18.7 us (31%)
  blocking collectives  13.6 us (23%)
  Pallas kernels  2.55 us (4%)
  local copies, waits for them, and re-layouts  0.98 us (2%)
  between operations  0.68 us (1%)
    ppermute x10, starting transfers between devices, send(): return lax.ppermute(array, ('core', 'z', 'xh', 'y'), pairs)  19.5 us
    all_to_all x1, blocking collectives, shards(): sums = lax.all_to_all(sums, ('core', 'z'), 0, 0)  13.6 us
    ppermute x10, waiting for transfers between devices, send(): return lax.ppermute(array, ('core', 'z', 'xh', 'y'), pairs)  10.4 us
    all_to_all x1, waiting for transfers between devices, shards(): sums = lax.all_to_all(sums, ('xl', 'xh', 'y'), 0, 0)  8.34 us
    all_to_all x1, starting transfers between devices, shards(): sums = lax.all_to_all(sums, ('xl', 'xh', 'y'), 0, 0)  3.48 us
    pallas_call x1, Pallas kernels, shards(): pl.pallas_call(best_kernel, out_shape=(jax.ShapeDtypeStruct((first, 1, ro...  1.83 us
  transfers between devices with their start and end apart: 11, of which 7 were waited for; matrix products, arithmetic and copies ran while one was open for 0% of the time, Pallas kernels for 0%

profile of v1, /device:TPU:1, one launch (start us, length us, event | category | flops | bytes accessed | tf_op | source)
XLA Modules:
  0.0 60.1 jit_solution(7475487790786858761)
XLA Ops:
  0.0 4.9 %collective-permute-start = (f32[128,512]{1,0:T(8,128)}, f32[128,512]{1,0:T(8,128)S(1)}, u32[]{:S(2)}, u32[]{:S(2)}) collective-permute-start(f32[128,512]{1,0:T(8,128)} %refs_0_.1), channel_id=1, source_target_pairs={{0,60},{1,61},{2,62},{3,63},{4,56},{5,57},{6,58},{7,59},{8,4},{9,5... | collective-permute-start | bytes 786440 | tf_op jit(solution)/shard_map/ppermute | solution.py:59
  4.9 8.0 %collective-permute-start.1 = (f32[128,512]{1,0:T(8,128)}, f32[128,512]{1,0:T(8,128)S(1)}, u32[]{:S(2)}, u32[]{:S(2)}) collective-permute-start(f32[128,512]{1,0:T(8,128)} %refs_0_.1), channel_id=1, source_target_pairs={{0,25},{1,26},{2,27},{3,24},{4,29},{5,30},{6,31},{7,28},{8,33},{9,... | collective-permute-start | bytes 786440 | tf_op jit(solution)/shard_map/ppermute | solution.py:59
  12.9 0.3 collective-permute-start.2
  13.3 0.0 copy-start
  13.3 1.0 %copy-done = f32[128,512]{1,0:T(8,128)S(1)} copy-done((f32[128,512]{1,0:T(8,128)S(1)}, f32[128,512]{1,0:T(8,128)}, u32[]{:S(2)}) %copy-start) | copy-done | bytes 262168
  14.3 13.6 %all_to_all.10.sums_ref = f32[16,1,512]{2,1,0:T(1,128)S(1)} all-to-all(f32[16,1,512]{2,1,0:T(1,128)S(1)} %shard_map.28), channel_id=1, replica_groups=mesh['xl'=2,'core'=2,'z'=8,'xh'=2,'y'=4] {'core','z'}, dimensions={0} | all-to-all | bytes 65536 | tf_op jit(solution)/shard_map/all_to_all | solution.py:154
  27.9 0.0 collective-permute-done.refs_1_
  27.9 0.0 collective-permute-done.1.refs_2_
  27.9 0.0 collective-permute-done.2.refs_3_
  27.9 0.7 %shard_map.29 = (f32[16,1,512]{2,1,0:T(1,128)}, f32[4,128,512]{2,1,0:T(8,128)S(1)}) custom-call(f32[16,1,512]{2,1,0:T(1,128)S(1)} %all_to_all.10.sums_ref, f32[128,512]{1,0:T(8,128)S(1)} %copy-done, f32[128,512]{1,0:T(8,128)S(1)} %collective-permute-done.refs_1_, f32[128,512]{1,0:T(8,128)S(1)} %collective-permute-done.1.refs_2_, ...), custom_call_target="tpu_custom_call" | custom-call | tf_op jit(solution)/shard_map/pallas_call | solution.py:155
  28.6 1.1 %collective-permute-start.3 = (f32[4,128,512]{2,1,0:T(8,128)S(1)}, f32[4,128,512]{2,1,0:T(8,128)S(1)}, u32[]{:S(2)}, u32[]{:S(2)}) collective-permute-start(f32[4,128,512]{2,1,0:T(8,128)S(1)} %get-tuple-element.15.refs_0_), channel_id=1, source_target_pairs={{0,1},{1,2},{2,3},{3,0},{4,5},{5,6},{6,7},{7,4},{8,9},{9,10},{10,1... | collective-permute-start | bytes 3145736 | tf_op jit(solution)/shard_map/ppermute | solution.py:59
  29.7 0.7 %collective-permute-start.4 = (f32[4,128,512]{2,1,0:T(8,128)S(1)}, f32[4,128,512]{2,1,0:T(8,128)S(1)}, u32[]{:S(2)}, u32[]{:S(2)}) collective-permute-start(f32[4,128,512]{2,1,0:T(8,128)S(1)} %get-tuple-element.15.refs_0_), channel_id=1, source_target_pairs={{0,8},{1,9},{2,10},{3,11},{4,12},{5,13},{6,14},{7,15},{8,16},{9,17... | collective-permute-start | bytes 3145736 | tf_op jit(solution)/shard_map/ppermute | solution.py:59
  30.4 3.5 %all-to-all-start.1 = ((f32[16,1,512]{2,1,0:T(1,128)}), f32[16,1,512]{2,1,0:T(1,128)S(1)}, u32[]{:S(2)}, u32[]{:S(2)}) async-start(f32[16,1,512]{2,1,0:T(1,128)} %get-tuple-element.14), calls=%async_computation.1 | async-start | bytes 65536 | tf_op jit(solution)/shard_map/all_to_all | solution.py:165
  34.6 8.3 %all-to-all-done.1.sums_ref = f32[16,1,512]{2,1,0:T(1,128)S(1)} async-done(((f32[16,1,512]{2,1,0:T(1,128)}), f32[16,1,512]{2,1,0:T(1,128)S(1)}, u32[]{:S(2)}, u32[]{:S(2)}) %all-to-all-start.1) | async-done | bytes 32800 | tf_op jit(solution)/shard_map/all_to_all | solution.py:165
  42.9 0.0 collective-permute-done.3.refs_1_
  42.9 0.7 %collective-permute-done.4.refs_2_ = f32[4,128,512]{2,1,0:T(8,128)S(1)} collective-permute-done((f32[4,128,512]{2,1,0:T(8,128)S(1)}, f32[4,128,512]{2,1,0:T(8,128)S(1)}, u32[]{:S(2)}, u32[]{:S(2)}) %collective-permute-start.4) | collective-permute-done | bytes 1048608 | tf_op jit(solution)/shard_map/ppermute | solution.py:59
  43.6 1.8 %shard_map.30 = (f32[4,1,128]{2,1,0:T(1,128)S(1)}, f32[4,1,128]{2,1,0:T(1,128)S(1)}, f32[4,1,128]{2,1,0:T(1,128)S(1)}) custom-call(s32[1]{0:T(128)} %copy.3.live_ref, f32[16,1,512]{2,1,0:T(1,128)S(1)} %all-to-all-done.1.sums_ref, f32[4,128,512]{2,1,0:T(8,128)S(1)} %get-tuple-element.15.refs_0_, f32[4,128,512]{2,1,0:T(8,128)S(1)} %collective-permute-done.3.refs_1_, ...), custom_call_target="tpu_custom_call" | custom-call | tf_op jit(solution)/shard_map/pallas_call | solution.py:167
  45.5 0.5 collective-permute-start.5
  45.9 0.5 collective-permute-start.6
  46.4 2.8 %collective-permute-done.5.refs_1_ = f32[4,1,128]{2,1,0:T(1,128)S(1)} collective-permute-done((f32[4,1,128]{2,1,0:T(1,128)S(1)}, f32[4,1,128]{2,1,0:T(1,128)S(1)}, u32[]{:S(2)}, u32[]{:S(2)}) %collective-permute-start.5) | collective-permute-done | bytes 2080 | tf_op jit(solution)/shard_map/ppermute | solution.py:59
  49.2 0.4 collective-permute-done.6.refs_2_
  49.6 1.6 %collective-permute-start.9 = (f32[1,128]{1,0:T(1,128)S(1)}, f32[1,128]{1,0:T(1,128)S(1)}, u32[]{:S(2)}, u32[]{:S(2)}) collective-permute-start(f32[1,128]{1,0:T(1,128)S(1)} %get-tuple-element.22), channel_id=1, source_target_pairs={{0,12},{1,13},{2,14},{3,15},{4,8},{5,9},{6,10},{7,11},{8,20},{9,21... | collective-permute-start | bytes 1544 | tf_op jit(solution)/shard_map/ppermute | solution.py:59
  51.2 0.9 %collective-permute-start.8 = (f32[1,128]{1,0:T(1,128)S(1)}, f32[1,128]{1,0:T(1,128)S(1)}, u32[]{:S(2)}, u32[]{:S(2)}) collective-permute-start(f32[1,128]{1,0:T(1,128)S(1)} %get-tuple-element.21), channel_id=1, source_target_pairs={{0,2},{1,3},{2,0},{3,1},{4,6},{5,7},{6,4},{7,5},{8,10},{9,11},{10,... | collective-permute-start | bytes 1544 | tf_op jit(solution)/shard_map/ppermute | solution.py:59
  52.0 1.0 %collective-permute-start.7 = (f32[1,128]{1,0:T(1,128)S(1)}, f32[1,128]{1,0:T(1,128)S(1)}, u32[]{:S(2)}, u32[]{:S(2)}) collective-permute-start(f32[1,128]{1,0:T(1,128)S(1)} %get-tuple-element.20), channel_id=1, source_target_pairs={{0,43},{1,40},{2,41},{3,42},{4,47},{5,44},{6,45},{7,46},{8,51},{9,... | collective-permute-start | bytes 1544 | tf_op jit(solution)/shard_map/ppermute | solution.py:59
  53.0 1.3 %collective-permute-done.9 = f32[1,128]{1,0:T(1,128)S(1)} collective-permute-done((f32[1,128]{1,0:T(1,128)S(1)}, f32[1,128]{1,0:T(1,128)S(1)}, u32[]{:S(2)}, u32[]{:S(2)}) %collective-permute-start.9) | collective-permute-done | bytes 544 | tf_op jit(solution)/shard_map/ppermute | solution.py:59
  54.4 0.7 %collective-permute-done.8 = f32[1,128]{1,0:T(1,128)S(1)} collective-permute-done((f32[1,128]{1,0:T(1,128)S(1)}, f32[1,128]{1,0:T(1,128)S(1)}, u32[]{:S(2)}, u32[]{:S(2)}) %collective-permute-start.8) | collective-permute-done | bytes 544 | tf_op jit(solution)/shard_map/ppermute | solution.py:59
  55.1 4.5 %collective-permute-done.7 = f32[1,128]{1,0:T(1,128)S(1)} collective-permute-done((f32[1,128]{1,0:T(1,128)S(1)}, f32[1,128]{1,0:T(1,128)S(1)}, u32[]{:S(2)}, u32[]{:S(2)}) %collective-permute-start.7) | collective-permute-done | bytes 544 | tf_op jit(solution)/shard_map/ppermute | solution.py:59
  59.5 0.5 compare_select_fusion
  (2 shorter events, 0.0 us)
Async XLA Ops:
  0.0 27.9 %collective-permute-start = (f32[128,512]{1,0:T(8,128)}, f32[128,512]{1,0:T(8,128)S(1)}, u32[]{:S(2)}, u32[]{:S(2)}) collective-permute-start(f32[128,512]{1,0:T(8,128)} %refs_0_.1), channel_id=1, source_target_pairs={{0,60},{1,61},{2,62},{3,63},{4,56},{5,57},{6,58},{7,59},{8,4},{9,5... | collective-permute-start | bytes 786440 | tf_op jit(solution)/shard_map/ppermute | solution.py:59
  4.9 23.0 %collective-permute-start.1 = (f32[128,512]{1,0:T(8,128)}, f32[128,512]{1,0:T(8,128)S(1)}, u32[]{:S(2)}, u32[]{:S(2)}) collective-permute-start(f32[128,512]{1,0:T(8,128)} %refs_0_.1), channel_id=1, source_target_pairs={{0,25},{1,26},{2,27},{3,24},{4,29},{5,30},{6,31},{7,28},{8,33},{9,... | collective-permute-start | bytes 786440 | tf_op jit(solution)/shard_map/ppermute | solution.py:59
  12.9 15.0 %collective-permute-start.2 = (f32[128,512]{1,0:T(8,128)}, f32[128,512]{1,0:T(8,128)S(1)}, u32[]{:S(2)}, u32[]{:S(2)}) collective-permute-start(f32[128,512]{1,0:T(8,128)} %refs_0_.1), channel_id=1, source_target_pairs={{0,2},{1,3},{2,0},{3,1},{4,6},{5,7},{6,4},{7,5},{8,10},{9,11},{10,... | collective-permute-start | bytes 786440 | tf_op jit(solution)/shard_map/ppermute | solution.py:59
  13.3 1.0 %copy-start = (f32[128,512]{1,0:T(8,128)S(1)}, f32[128,512]{1,0:T(8,128)}, u32[]{:S(2)}) copy-start(f32[128,512]{1,0:T(8,128)} %refs_0_.1) | copy-start | bytes 786436
  28.6 14.3 %collective-permute-start.3 = (f32[4,128,512]{2,1,0:T(8,128)S(1)}, f32[4,128,512]{2,1,0:T(8,128)S(1)}, u32[]{:S(2)}, u32[]{:S(2)}) collective-permute-start(f32[4,128,512]{2,1,0:T(8,128)S(1)} %get-tuple-element.15.refs_0_), channel_id=1, source_target_pairs={{0,1},{1,2},{2,3},{3,0},{4,5},{5,6},{6,7},{7,4},{8,9},{9,10},{10,1... | collective-permute-start | bytes 3145736 | tf_op jit(solution)/shard_map/ppermute | solution.py:59
  29.7 13.9 %collective-permute-start.4 = (f32[4,128,512]{2,1,0:T(8,128)S(1)}, f32[4,128,512]{2,1,0:T(8,128)S(1)}, u32[]{:S(2)}, u32[]{:S(2)}) collective-permute-start(f32[4,128,512]{2,1,0:T(8,128)S(1)} %get-tuple-element.15.refs_0_), channel_id=1, source_target_pairs={{0,8},{1,9},{2,10},{3,11},{4,12},{5,13},{6,14},{7,15},{8,16},{9,17... | collective-permute-start | bytes 3145736 | tf_op jit(solution)/shard_map/ppermute | solution.py:59
  30.4 12.5 %all-to-all-start.1 = ((f32[16,1,512]{2,1,0:T(1,128)}), f32[16,1,512]{2,1,0:T(1,128)S(1)}, u32[]{:S(2)}, u32[]{:S(2)}) async-start(f32[16,1,512]{2,1,0:T(1,128)} %get-tuple-element.14), calls=%async_computation.1 | async-start | bytes 65536 | tf_op jit(solution)/shard_map/all_to_all | solution.py:165
  45.5 3.7 %collective-permute-start.5 = (f32[4,1,128]{2,1,0:T(1,128)S(1)}, f32[4,1,128]{2,1,0:T(1,128)S(1)}, u32[]{:S(2)}, u32[]{:S(2)}) collective-permute-start(f32[4,1,128]{2,1,0:T(1,128)S(1)} %get-tuple-element.17), channel_id=1, source_target_pairs={{0,3},{1,0},{2,1},{3,2},{4,7},{5,4},{6,5},{7,6},{8,11},{9,8},{10,9... | collective-permute-start | bytes 6152 | tf_op jit(solution)/shard_map/ppermute | solution.py:59
  45.9 3.6 %collective-permute-start.6 = (f32[4,1,128]{2,1,0:T(1,128)S(1)}, f32[4,1,128]{2,1,0:T(1,128)S(1)}, u32[]{:S(2)}, u32[]{:S(2)}) collective-permute-start(f32[4,1,128]{2,1,0:T(1,128)S(1)} %get-tuple-element.18), channel_id=1, source_target_pairs={{0,56},{1,57},{2,58},{3,59},{4,60},{5,61},{6,62},{7,63},{8,0},{9,1... | collective-permute-start | bytes 6152 | tf_op jit(solution)/shard_map/ppermute | solution.py:59
  49.6 4.8 %collective-permute-start.9 = (f32[1,128]{1,0:T(1,128)S(1)}, f32[1,128]{1,0:T(1,128)S(1)}, u32[]{:S(2)}, u32[]{:S(2)}) collective-permute-start(f32[1,128]{1,0:T(1,128)S(1)} %get-tuple-element.22), channel_id=1, source_target_pairs={{0,12},{1,13},{2,14},{3,15},{4,8},{5,9},{6,10},{7,11},{8,20},{9,21... | collective-permute-start | bytes 1544 | tf_op jit(solution)/shard_map/ppermute | solution.py:59
  51.2 3.9 %collective-permute-start.8 = (f32[1,128]{1,0:T(1,128)S(1)}, f32[1,128]{1,0:T(1,128)S(1)}, u32[]{:S(2)}, u32[]{:S(2)}) collective-permute-start(f32[1,128]{1,0:T(1,128)S(1)} %get-tuple-element.21), channel_id=1, source_target_pairs={{0,2},{1,3},{2,0},{3,1},{4,6},{5,7},{6,4},{7,5},{8,10},{9,11},{10,... | collective-permute-start | bytes 1544 | tf_op jit(solution)/shard_map/ppermute | solution.py:59
  52.0 7.5 %collective-permute-start.7 = (f32[1,128]{1,0:T(1,128)S(1)}, f32[1,128]{1,0:T(1,128)S(1)}, u32[]{:S(2)}, u32[]{:S(2)}) collective-permute-start(f32[1,128]{1,0:T(1,128)S(1)} %get-tuple-element.20), channel_id=1, source_target_pairs={{0,43},{1,40},{2,41},{3,42},{4,47},{5,44},{6,45},{7,46},{8,51},{9,... | collective-permute-start | bytes 1544 | tf_op jit(solution)/shard_map/ppermute | solution.py:59

commit v2 on v1

--- a/solution.py
+++ b/solution.py
@@ -59,7 +59,8 @@
     return lax.ppermute(array, ("core", "z", "xh", "y"), pairs)
 
 
-def head_kernel(own_ref, sums_ref):
+def head_kernel(live_ref, own_ref, sums_ref, count_ref):
+    count_ref[...] = jnp.full(count_ref.shape, live_ref[0], jnp.int32)
     sums_ref[...] = jnp.broadcast_to(
         jnp.sum(own_ref[...], axis=0, keepdims=True)[None], sums_ref.shape
     )
@@ -86,7 +87,7 @@
     rows = held[0].shape[1]
     per = len(FIRST)
     centre = jnp.sum(sums_ref[...], axis=0) / (rows * 4 * BLOCKS)
-    live = live_ref[0]
+    live = live_ref[...]
     core = lax.axis_index("core")
     at = [lax.axis_index(a) for a in ("z", "xh", "y")]
     lane = lax.broadcasted_iota(jnp.int32, (1, rows), 1)
@@ -144,13 +145,16 @@
     small = pltpu.CompilerParams(vmem_limit_bytes=4 * 1024 * 1024)
     first, second = len(FIRST), len(SECOND)
     arrived = [send(embeddings, step, 1) for step in FIRST[1:]]
-    sums = pl.pallas_call(
+    sums, count = pl.pallas_call(
         head_kernel,
-        out_shape=jax.ShapeDtypeStruct((16, 1, width), jnp.float32),
-        in_specs=[vmem],
-        out_specs=vmem,
+        out_shape=(
+            jax.ShapeDtypeStruct((16, 1, width), jnp.float32),
+            jax.ShapeDtypeStruct((1, rows), jnp.int32),
+        ),
+        in_specs=[pl.BlockSpec(memory_space=pltpu.SMEM), vmem],
+        out_specs=(vmem, vmem),
         compiler_params=small,
-    )(embeddings)
+    )(cluster_sizes, embeddings)
     sums = lax.all_to_all(sums, ("core", "z"), 0, 0)
     sums, held = pl.pallas_call(
         middle_kernel,
@@ -167,11 +171,11 @@
     found = pl.pallas_call(
         best_kernel,
         out_shape=(jax.ShapeDtypeStruct((first, 1, rows), jnp.float32),) * second,
-        in_specs=[pl.BlockSpec(memory_space=pltpu.SMEM)] + [vmem] * (second + 1),
+        in_specs=[vmem] * (second + 2),
         out_specs=(vmem,) * second,
         scratch_shapes=[pltpu.VMEM((first * second, rows, width), jnp.bfloat16)],
         compiler_params=pltpu.CompilerParams(vmem_limit_bytes=20 * 1024 * 1024),
-    )(cluster_sizes, sums, *held)
+    )(count, sums, *held)
     back = [send(f, step, -1) for f, step in zip(found[1:], SECOND[1:])]
     lines = pl.pallas_call(
         merge_kernel,
@@ -185,7 +189,7 @@
         best = jnp.maximum(best, send(lines[k], FIRST[k], -1))
     block = lax.axis_index("z") * 8 + lax.axis_index("xh") * 4 + lax.axis_index("y")
     row_ids = block * rows + jnp.arange(rows, dtype=jnp.int32)
-    return jnp.where(row_ids < cluster_sizes[0], best[0], jnp.float32(0.0))
+    return jnp.where(row_ids < count[0], best[0], jnp.float32(0.0))
 
 
 def solution(mesh):

time: 60.3 us -> 60.4 us (level)
  blocking collectives: 13.6 us -> 26.1 us
  waiting for transfers between devices: 18.7 us -> 10.4 us
  starting transfers between devices: 23 us -> 19.6 us
    all_to_all x0 -> x1, blocking collectives: none -> 12.5 us  [shards(): sums = lax.all_to_all(sums, ('xl', 'xh', 'y'), 0, 0)]
    all_to_all x1 -> x0, waiting for transfers between devices: 8.34 us -> none  [shards(): sums = lax.all_to_all(sums, ('xl', 'xh', 'y'), 0, 0)]
    all_to_all x1 -> x0, starting transfers between devices: 3.48 us -> none  [shards(): sums = lax.all_to_all(sums, ('xl', 'xh', 'y'), 0, 0)]
  transfers between devices with their start and end apart: 11 -> 10, of which waited for: 7 -> 6; matrix products, arithmetic and copies ran while one was open for 0% -> 0% of each run, Pallas kernels for 0% -> 0%
where the time goes in v2:
time: 60.4 us; the launch traced here: 60.2 us
  blocking collectives  26.1 us (43%)
  starting transfers between devices  19.6 us (32%)
  waiting for transfers between devices  10.4 us (17%)
  Pallas kernels  1.99 us (3%)
  local copies, waits for them, and re-layouts  0.94 us (2%)
  between operations  0.69 us (1%)
    ppermute x10, starting transfers between devices, send(): return lax.ppermute(array, ('core', 'z', 'xh', 'y'), pairs)  19.6 us
    all_to_all x1, blocking collectives, shards(): sums = lax.all_to_all(sums, ('core', 'z'), 0, 0)  13.6 us
    all_to_all x1, blocking collectives, shards(): sums = lax.all_to_all(sums, ('xl', 'xh', 'y'), 0, 0)  12.5 us
    ppermute x10, waiting for transfers between devices, send(): return lax.ppermute(array, ('core', 'z', 'xh', 'y'), pairs)  10.4 us
    pallas_call x1, Pallas kernels, shards(): pl.pallas_call(best_kernel, out_shape=(jax.ShapeDtypeStruct((first, 1, ro...  1.86 us
  transfers between devices with their start and end apart: 10, of which 6 were waited for; matrix products, arithmetic and copies ran while one was open for 0% of the time, Pallas kernels for 0%

profile of v2, /device:TPU:1, one launch (start us, length us, event | category | flops | bytes accessed | tf_op | source)
XLA Modules:
  0.0 60.2 jit_solution(14678344427042907166)
XLA Ops:
  0.0 4.9 %collective-permute-start = (f32[128,512]{1,0:T(8,128)}, f32[128,512]{1,0:T(8,128)S(1)}, u32[]{:S(2)}, u32[]{:S(2)}) collective-permute-start(f32[128,512]{1,0:T(8,128)} %refs_0_.1), channel_id=1, source_target_pairs={{0,60},{1,61},{2,62},{3,63},{4,56},{5,57},{6,58},{7,59},{8,4},{9,5... | collective-permute-start | bytes 786440 | tf_op jit(solution)/shard_map/ppermute | solution.py:59
  4.9 8.0 %collective-permute-start.1 = (f32[128,512]{1,0:T(8,128)}, f32[128,512]{1,0:T(8,128)S(1)}, u32[]{:S(2)}, u32[]{:S(2)}) collective-permute-start(f32[128,512]{1,0:T(8,128)} %refs_0_.1), channel_id=1, source_target_pairs={{0,25},{1,26},{2,27},{3,24},{4,29},{5,30},{6,31},{7,28},{8,33},{9,... | collective-permute-start | bytes 786440 | tf_op jit(solution)/shard_map/ppermute | solution.py:59
  12.9 0.3 collective-permute-start.2
  13.9 0.0 copy-start
  14.0 0.9 %copy-done = f32[128,512]{1,0:T(8,128)S(1)} copy-done((f32[128,512]{1,0:T(8,128)S(1)}, f32[128,512]{1,0:T(8,128)}, u32[]{:S(2)}) %copy-start) | copy-done | bytes 262168
  14.9 13.6 %all_to_all.10.sums_ref = f32[16,1,512]{2,1,0:T(1,128)S(1)} all-to-all(f32[16,1,512]{2,1,0:T(1,128)S(1)} %get-tuple-element.17), channel_id=1, replica_groups=mesh['xl'=2,'core'=2,'z'=8,'xh'=2,'y'=4] {'core','z'}, dimensions={0} | all-to-all | bytes 65536 | tf_op jit(solution)/shard_map/all_to_all | solution.py:158
  28.5 0.0 collective-permute-done.refs_1_
  28.5 0.0 collective-permute-done.1.refs_2_
  28.5 0.0 collective-permute-done.2.refs_3_
  28.6 0.1 shard_map.29
  28.6 1.1 %collective-permute-start.3 = (f32[4,128,512]{2,1,0:T(8,128)S(1)}, f32[4,128,512]{2,1,0:T(8,128)S(1)}, u32[]{:S(2)}, u32[]{:S(2)}) collective-permute-start(f32[4,128,512]{2,1,0:T(8,128)S(1)} %get-tuple-element.19.refs_0_), channel_id=1, source_target_pairs={{0,1},{1,2},{2,3},{3,0},{4,5},{5,6},{6,7},{7,4},{8,9},{9,10},{10,1... | collective-permute-start | bytes 3145736 | tf_op jit(solution)/shard_map/ppermute | solution.py:59
  29.8 0.7 %collective-permute-start.4 = (f32[4,128,512]{2,1,0:T(8,128)S(1)}, f32[4,128,512]{2,1,0:T(8,128)S(1)}, u32[]{:S(2)}, u32[]{:S(2)}) collective-permute-start(f32[4,128,512]{2,1,0:T(8,128)S(1)} %get-tuple-element.19.refs_0_), channel_id=1, source_target_pairs={{0,8},{1,9},{2,10},{3,11},{4,12},{5,13},{6,14},{7,15},{8,16},{9,17... | collective-permute-start | bytes 3145736 | tf_op jit(solution)/shard_map/ppermute | solution.py:59
  30.5 12.5 %all_to_all.11.sums_ref = f32[16,1,512]{2,1,0:T(1,128)S(1)} all-to-all(f32[16,1,512]{2,1,0:T(1,128)S(1)} %get-tuple-element.18), channel_id=1, replica_groups=mesh['xl'=2,'core'=2,'z'=8,'xh'=2,'y'=4] {'xl','xh','y'}, dimensions={0} | all-to-all | bytes 65536 | tf_op jit(solution)/shard_map/all_to_all | solution.py:169
  43.0 0.0 collective-permute-done.3.refs_1_
  43.0 0.7 %collective-permute-done.4.refs_2_ = f32[4,128,512]{2,1,0:T(8,128)S(1)} collective-permute-done((f32[4,128,512]{2,1,0:T(8,128)S(1)}, f32[4,128,512]{2,1,0:T(8,128)S(1)}, u32[]{:S(2)}, u32[]{:S(2)}) %collective-permute-start.4) | collective-permute-done | bytes 1048608 | tf_op jit(solution)/shard_map/ppermute | solution.py:59
  43.7 1.9 %shard_map.30 = (f32[4,1,128]{2,1,0:T(1,128)S(1)}, f32[4,1,128]{2,1,0:T(1,128)S(1)}, f32[4,1,128]{2,1,0:T(1,128)S(1)}) custom-call(s32[1,128]{1,0:T(1,128)S(1)} %get-tuple-element.16.live_ref, f32[16,1,512]{2,1,0:T(1,128)S(1)} %all_to_all.11.sums_ref, f32[4,128,512]{2,1,0:T(8,128)S(1)} %get-tuple-element.19.refs_0_, ...), custom_call_target="tpu_custom_call" | custom-call | tf_op jit(solution)/shard_map/pallas_call | solution.py:171
  45.6 0.5 collective-permute-start.5
  46.1 0.5 collective-permute-start.6
  46.6 2.8 %collective-permute-done.5.refs_1_ = f32[4,1,128]{2,1,0:T(1,128)S(1)} collective-permute-done((f32[4,1,128]{2,1,0:T(1,128)S(1)}, f32[4,1,128]{2,1,0:T(1,128)S(1)}, u32[]{:S(2)}, u32[]{:S(2)}) %collective-permute-start.5) | collective-permute-done | bytes 2080 | tf_op jit(solution)/shard_map/ppermute | solution.py:59
  49.3 0.4 collective-permute-done.6.refs_2_
  49.7 1.6 %collective-permute-start.9 = (f32[1,128]{1,0:T(1,128)S(1)}, f32[1,128]{1,0:T(1,128)S(1)}, u32[]{:S(2)}, u32[]{:S(2)}) collective-permute-start(f32[1,128]{1,0:T(1,128)S(1)} %get-tuple-element.26), channel_id=1, source_target_pairs={{0,12},{1,13},{2,14},{3,15},{4,8},{5,9},{6,10},{7,11},{8,20},{9,21... | collective-permute-start | bytes 1544 | tf_op jit(solution)/shard_map/ppermute | solution.py:59
  51.3 0.9 %collective-permute-start.8 = (f32[1,128]{1,0:T(1,128)S(1)}, f32[1,128]{1,0:T(1,128)S(1)}, u32[]{:S(2)}, u32[]{:S(2)}) collective-permute-start(f32[1,128]{1,0:T(1,128)S(1)} %get-tuple-element.25), channel_id=1, source_target_pairs={{0,2},{1,3},{2,0},{3,1},{4,6},{5,7},{6,4},{7,5},{8,10},{9,11},{10,... | collective-permute-start | bytes 1544 | tf_op jit(solution)/shard_map/ppermute | solution.py:59
  52.2 1.0 %collective-permute-start.7 = (f32[1,128]{1,0:T(1,128)S(1)}, f32[1,128]{1,0:T(1,128)S(1)}, u32[]{:S(2)}, u32[]{:S(2)}) collective-permute-start(f32[1,128]{1,0:T(1,128)S(1)} %get-tuple-element.24), channel_id=1, source_target_pairs={{0,43},{1,40},{2,41},{3,42},{4,47},{5,44},{6,45},{7,46},{8,51},{9,... | collective-permute-start | bytes 1544 | tf_op jit(solution)/shard_map/ppermute | solution.py:59
  53.2 1.4 %collective-permute-done.9 = f32[1,128]{1,0:T(1,128)S(1)} collective-permute-done((f32[1,128]{1,0:T(1,128)S(1)}, f32[1,128]{1,0:T(1,128)S(1)}, u32[]{:S(2)}, u32[]{:S(2)}) %collective-permute-start.9) | collective-permute-done | bytes 544 | tf_op jit(solution)/shard_map/ppermute | solution.py:59
  54.5 0.7 %collective-permute-done.8 = f32[1,128]{1,0:T(1,128)S(1)} collective-permute-done((f32[1,128]{1,0:T(1,128)S(1)}, f32[1,128]{1,0:T(1,128)S(1)}, u32[]{:S(2)}, u32[]{:S(2)}) %collective-permute-start.8) | collective-permute-done | bytes 544 | tf_op jit(solution)/shard_map/ppermute | solution.py:59
  55.2 4.5 %collective-permute-done.7 = f32[1,128]{1,0:T(1,128)S(1)} collective-permute-done((f32[1,128]{1,0:T(1,128)S(1)}, f32[1,128]{1,0:T(1,128)S(1)}, u32[]{:S(2)}, u32[]{:S(2)}) %collective-permute-start.7) | collective-permute-done | bytes 544 | tf_op jit(solution)/shard_map/ppermute | solution.py:59
  59.7 0.5 compare_select_fusion
  (2 shorter events, 0.0 us)
Async XLA Ops:
  0.0 28.5 %collective-permute-start = (f32[128,512]{1,0:T(8,128)}, f32[128,512]{1,0:T(8,128)S(1)}, u32[]{:S(2)}, u32[]{:S(2)}) collective-permute-start(f32[128,512]{1,0:T(8,128)} %refs_0_.1), channel_id=1, source_target_pairs={{0,60},{1,61},{2,62},{3,63},{4,56},{5,57},{6,58},{7,59},{8,4},{9,5... | collective-permute-start | bytes 786440 | tf_op jit(solution)/shard_map/ppermute | solution.py:59
  4.9 23.6 %collective-permute-start.1 = (f32[128,512]{1,0:T(8,128)}, f32[128,512]{1,0:T(8,128)S(1)}, u32[]{:S(2)}, u32[]{:S(2)}) collective-permute-start(f32[128,512]{1,0:T(8,128)} %refs_0_.1), channel_id=1, source_target_pairs={{0,25},{1,26},{2,27},{3,24},{4,29},{5,30},{6,31},{7,28},{8,33},{9,... | collective-permute-start | bytes 786440 | tf_op jit(solution)/shard_map/ppermute | solution.py:59
  12.9 15.6 %collective-permute-start.2 = (f32[128,512]{1,0:T(8,128)}, f32[128,512]{1,0:T(8,128)S(1)}, u32[]{:S(2)}, u32[]{:S(2)}) collective-permute-start(f32[128,512]{1,0:T(8,128)} %refs_0_.1), channel_id=1, source_target_pairs={{0,2},{1,3},{2,0},{3,1},{4,6},{5,7},{6,4},{7,5},{8,10},{9,11},{10,... | collective-permute-start | bytes 786440 | tf_op jit(solution)/shard_map/ppermute | solution.py:59
  13.9 1.0 %copy-start = (f32[128,512]{1,0:T(8,128)S(1)}, f32[128,512]{1,0:T(8,128)}, u32[]{:S(2)}) copy-start(f32[128,512]{1,0:T(8,128)} %refs_0_.1) | copy-start | bytes 786436
  28.6 14.4 %collective-permute-start.3 = (f32[4,128,512]{2,1,0:T(8,128)S(1)}, f32[4,128,512]{2,1,0:T(8,128)S(1)}, u32[]{:S(2)}, u32[]{:S(2)}) collective-permute-start(f32[4,128,512]{2,1,0:T(8,128)S(1)} %get-tuple-element.19.refs_0_), channel_id=1, source_target_pairs={{0,1},{1,2},{2,3},{3,0},{4,5},{5,6},{6,7},{7,4},{8,9},{9,10},{10,1... | collective-permute-start | bytes 3145736 | tf_op jit(solution)/shard_map/ppermute | solution.py:59
  29.8 13.9 %collective-permute-start.4 = (f32[4,128,512]{2,1,0:T(8,128)S(1)}, f32[4,128,512]{2,1,0:T(8,128)S(1)}, u32[]{:S(2)}, u32[]{:S(2)}) collective-permute-start(f32[4,128,512]{2,1,0:T(8,128)S(1)} %get-tuple-element.19.refs_0_), channel_id=1, source_target_pairs={{0,8},{1,9},{2,10},{3,11},{4,12},{5,13},{6,14},{7,15},{8,16},{9,17... | collective-permute-start | bytes 3145736 | tf_op jit(solution)/shard_map/ppermute | solution.py:59
  45.6 3.7 %collective-permute-start.5 = (f32[4,1,128]{2,1,0:T(1,128)S(1)}, f32[4,1,128]{2,1,0:T(1,128)S(1)}, u32[]{:S(2)}, u32[]{:S(2)}) collective-permute-start(f32[4,1,128]{2,1,0:T(1,128)S(1)} %get-tuple-element.21), channel_id=1, source_target_pairs={{0,3},{1,0},{2,1},{3,2},{4,7},{5,4},{6,5},{7,6},{8,11},{9,8},{10,9... | collective-permute-start | bytes 6152 | tf_op jit(solution)/shard_map/ppermute | solution.py:59
  46.1 3.6 %collective-permute-start.6 = (f32[4,1,128]{2,1,0:T(1,128)S(1)}, f32[4,1,128]{2,1,0:T(1,128)S(1)}, u32[]{:S(2)}, u32[]{:S(2)}) collective-permute-start(f32[4,1,128]{2,1,0:T(1,128)S(1)} %get-tuple-element.22), channel_id=1, source_target_pairs={{0,56},{1,57},{2,58},{3,59},{4,60},{5,61},{6,62},{7,63},{8,0},{9,1... | collective-permute-start | bytes 6152 | tf_op jit(solution)/shard_map/ppermute | solution.py:59
  49.7 4.8 %collective-permute-start.9 = (f32[1,128]{1,0:T(1,128)S(1)}, f32[1,128]{1,0:T(1,128)S(1)}, u32[]{:S(2)}, u32[]{:S(2)}) collective-permute-start(f32[1,128]{1,0:T(1,128)S(1)} %get-tuple-element.26), channel_id=1, source_target_pairs={{0,12},{1,13},{2,14},{3,15},{4,8},{5,9},{6,10},{7,11},{8,20},{9,21... | collective-permute-start | bytes 1544 | tf_op jit(solution)/shard_map/ppermute | solution.py:59
  51.3 3.9 %collective-permute-start.8 = (f32[1,128]{1,0:T(1,128)S(1)}, f32[1,128]{1,0:T(1,128)S(1)}, u32[]{:S(2)}, u32[]{:S(2)}) collective-permute-start(f32[1,128]{1,0:T(1,128)S(1)} %get-tuple-element.25), channel_id=1, source_target_pairs={{0,2},{1,3},{2,0},{3,1},{4,6},{5,7},{6,4},{7,5},{8,10},{9,11},{10,... | collective-permute-start | bytes 1544 | tf_op jit(solution)/shard_map/ppermute | solution.py:59
  52.2 7.5 %collective-permute-start.7 = (f32[1,128]{1,0:T(1,128)S(1)}, f32[1,128]{1,0:T(1,128)S(1)}, u32[]{:S(2)}, u32[]{:S(2)}) collective-permute-start(f32[1,128]{1,0:T(1,128)S(1)} %get-tuple-element.24), channel_id=1, source_target_pairs={{0,43},{1,40},{2,41},{3,42},{4,47},{5,44},{6,45},{7,46},{8,51},{9,... | collective-permute-start | bytes 1544 | tf_op jit(solution)/shard_map/ppermute | solution.py:59

commit v3 on v1

--- a/solution.py
+++ b/solution.py
@@ -163,7 +163,8 @@
         compiler_params=small,
     )(sums, embeddings, *arrived)
     sums = lax.all_to_all(sums, ("xl", "xh", "y"), 0, 0)
-    held = [held] + [send(held, step, 1) for step in SECOND[1:]]
+    far = send(held, SECOND[2], 1)
+    held = [held, send(held, SECOND[1], 1), far]
     found = pl.pallas_call(
         best_kernel,
         out_shape=(jax.ShapeDtypeStruct((first, 1, rows), jnp.float32),) * second,

time: 60.3 us -> 60.3 us (level)
  no operation moved by 1% of the time
where the time goes in v3:
time: 60.3 us; the launch traced here: 60.1 us
  starting transfers between devices  23 us (38%)
  waiting for transfers between devices  18.7 us (31%)
  blocking collectives  13.6 us (23%)
  Pallas kernels  2.55 us (4%)
  local copies, waits for them, and re-layouts  0.98 us (2%)
  between operations  0.68 us (1%)
    ppermute x10, starting transfers between devices, send(): return lax.ppermute(array, ('core', 'z', 'xh', 'y'), pairs)  19.5 us
    all_to_all x1, blocking collectives, shards(): sums = lax.all_to_all(sums, ('core', 'z'), 0, 0)  13.6 us
    ppermute x10, waiting for transfers between devices, send(): return lax.ppermute(array, ('core', 'z', 'xh', 'y'), pairs)  10.4 us
    all_to_all x1, waiting for transfers between devices, shards(): sums = lax.all_to_all(sums, ('xl', 'xh', 'y'), 0, 0)  8.34 us
    all_to_all x1, starting transfers between devices, shards(): sums = lax.all_to_all(sums, ('xl', 'xh', 'y'), 0, 0)  3.48 us
    pallas_call x1, Pallas kernels, shards(): pl.pallas_call(best_kernel, out_shape=(jax.ShapeDtypeStruct((first, 1, ro...  1.83 us
  transfers between devices with their start and end apart: 11, of which 7 were waited for; matrix products, arithmetic and copies ran while one was open for 0% of the time, Pallas kernels for 0%

profile of v3, /device:TPU:1, one launch (start us, length us, event | category | flops | bytes accessed | tf_op | source)
XLA Modules:
  0.0 60.1 jit_solution(7475487790786858761)
XLA Ops:
  0.0 4.9 %collective-permute-start = (f32[128,512]{1,0:T(8,128)}, f32[128,512]{1,0:T(8,128)S(1)}, u32[]{:S(2)}, u32[]{:S(2)}) collective-permute-start(f32[128,512]{1,0:T(8,128)} %refs_0_.1), channel_id=1, source_target_pairs={{0,60},{1,61},{2,62},{3,63},{4,56},{5,57},{6,58},{7,59},{8,4},{9,5... | collective-permute-start | bytes 786440 | tf_op jit(solution)/shard_map/ppermute | solution.py:59
  4.9 8.0 %collective-permute-start.1 = (f32[128,512]{1,0:T(8,128)}, f32[128,512]{1,0:T(8,128)S(1)}, u32[]{:S(2)}, u32[]{:S(2)}) collective-permute-start(f32[128,512]{1,0:T(8,128)} %refs_0_.1), channel_id=1, source_target_pairs={{0,25},{1,26},{2,27},{3,24},{4,29},{5,30},{6,31},{7,28},{8,33},{9,... | collective-permute-start | bytes 786440 | tf_op jit(solution)/shard_map/ppermute | solution.py:59
  12.9 0.3 collective-permute-start.2
  13.3 0.0 copy-start
  13.3 1.0 %copy-done = f32[128,512]{1,0:T(8,128)S(1)} copy-done((f32[128,512]{1,0:T(8,128)S(1)}, f32[128,512]{1,0:T(8,128)}, u32[]{:S(2)}) %copy-start) | copy-done | bytes 262168
  14.3 13.6 %all_to_all.10.sums_ref = f32[16,1,512]{2,1,0:T(1,128)S(1)} all-to-all(f32[16,1,512]{2,1,0:T(1,128)S(1)} %shard_map.28), channel_id=1, replica_groups=mesh['xl'=2,'core'=2,'z'=8,'xh'=2,'y'=4] {'core','z'}, dimensions={0} | all-to-all | bytes 65536 | tf_op jit(solution)/shard_map/all_to_all | solution.py:154
  27.9 0.0 collective-permute-done.refs_1_
  27.9 0.0 collective-permute-done.1.refs_2_
  27.9 0.0 collective-permute-done.2.refs_3_
  27.9 0.7 %shard_map.29 = (f32[16,1,512]{2,1,0:T(1,128)}, f32[4,128,512]{2,1,0:T(8,128)S(1)}) custom-call(f32[16,1,512]{2,1,0:T(1,128)S(1)} %all_to_all.10.sums_ref, f32[128,512]{1,0:T(8,128)S(1)} %copy-done, f32[128,512]{1,0:T(8,128)S(1)} %collective-permute-done.refs_1_, f32[128,512]{1,0:T(8,128)S(1)} %collective-permute-done.1.refs_2_, ...), custom_call_target="tpu_custom_call" | custom-call | tf_op jit(solution)/shard_map/pallas_call | solution.py:155
  28.6 1.1 %collective-permute-start.3 = (f32[4,128,512]{2,1,0:T(8,128)S(1)}, f32[4,128,512]{2,1,0:T(8,128)S(1)}, u32[]{:S(2)}, u32[]{:S(2)}) collective-permute-start(f32[4,128,512]{2,1,0:T(8,128)S(1)} %get-tuple-element.15.refs_0_), channel_id=1, source_target_pairs={{0,1},{1,2},{2,3},{3,0},{4,5},{5,6},{6,7},{7,4},{8,9},{9,10},{10,1... | collective-permute-start | bytes 3145736 | tf_op jit(solution)/shard_map/ppermute | solution.py:59
  29.7 0.7 %collective-permute-start.4 = (f32[4,128,512]{2,1,0:T(8,128)S(1)}, f32[4,128,512]{2,1,0:T(8,128)S(1)}, u32[]{:S(2)}, u32[]{:S(2)}) collective-permute-start(f32[4,128,512]{2,1,0:T(8,128)S(1)} %get-tuple-element.15.refs_0_), channel_id=1, source_target_pairs={{0,8},{1,9},{2,10},{3,11},{4,12},{5,13},{6,14},{7,15},{8,16},{9,17... | collective-permute-start | bytes 3145736 | tf_op jit(solution)/shard_map/ppermute | solution.py:59
  30.4 3.5 %all-to-all-start.1 = ((f32[16,1,512]{2,1,0:T(1,128)}), f32[16,1,512]{2,1,0:T(1,128)S(1)}, u32[]{:S(2)}, u32[]{:S(2)}) async-start(f32[16,1,512]{2,1,0:T(1,128)} %get-tuple-element.14), calls=%async_computation.1 | async-start | bytes 65536 | tf_op jit(solution)/shard_map/all_to_all | solution.py:165
  34.6 8.3 %all-to-all-done.1.sums_ref = f32[16,1,512]{2,1,0:T(1,128)S(1)} async-done(((f32[16,1,512]{2,1,0:T(1,128)}), f32[16,1,512]{2,1,0:T(1,128)S(1)}, u32[]{:S(2)}, u32[]{:S(2)}) %all-to-all-start.1) | async-done | bytes 32800 | tf_op jit(solution)/shard_map/all_to_all | solution.py:165
  42.9 0.0 collective-permute-done.3.refs_1_
  42.9 0.7 %collective-permute-done.4.refs_2_ = f32[4,128,512]{2,1,0:T(8,128)S(1)} collective-permute-done((f32[4,128,512]{2,1,0:T(8,128)S(1)}, f32[4,128,512]{2,1,0:T(8,128)S(1)}, u32[]{:S(2)}, u32[]{:S(2)}) %collective-permute-start.4) | collective-permute-done | bytes 1048608 | tf_op jit(solution)/shard_map/ppermute | solution.py:59
  43.6 1.8 %shard_map.30 = (f32[4,1,128]{2,1,0:T(1,128)S(1)}, f32[4,1,128]{2,1,0:T(1,128)S(1)}, f32[4,1,128]{2,1,0:T(1,128)S(1)}) custom-call(s32[1]{0:T(128)} %copy.3.live_ref, f32[16,1,512]{2,1,0:T(1,128)S(1)} %all-to-all-done.1.sums_ref, f32[4,128,512]{2,1,0:T(8,128)S(1)} %get-tuple-element.15.refs_0_, f32[4,128,512]{2,1,0:T(8,128)S(1)} %collective-permute-done.3.refs_1_, ...), custom_call_target="tpu_custom_call" | custom-call | tf_op jit(solution)/shard_map/pallas_call | solution.py:168
  45.5 0.5 collective-permute-start.5
  45.9 0.5 collective-permute-start.6
  46.4 2.8 %collective-permute-done.5.refs_1_ = f32[4,1,128]{2,1,0:T(1,128)S(1)} collective-permute-done((f32[4,1,128]{2,1,0:T(1,128)S(1)}, f32[4,1,128]{2,1,0:T(1,128)S(1)}, u32[]{:S(2)}, u32[]{:S(2)}) %collective-permute-start.5) | collective-permute-done | bytes 2080 | tf_op jit(solution)/shard_map/ppermute | solution.py:59
  49.2 0.4 collective-permute-done.6.refs_2_
  49.6 1.6 %collective-permute-start.9 = (f32[1,128]{1,0:T(1,128)S(1)}, f32[1,128]{1,0:T(1,128)S(1)}, u32[]{:S(2)}, u32[]{:S(2)}) collective-permute-start(f32[1,128]{1,0:T(1,128)S(1)} %get-tuple-element.22), channel_id=1, source_target_pairs={{0,12},{1,13},{2,14},{3,15},{4,8},{5,9},{6,10},{7,11},{8,20},{9,21... | collective-permute-start | bytes 1544 | tf_op jit(solution)/shard_map/ppermute | solution.py:59
  51.2 0.9 %collective-permute-start.8 = (f32[1,128]{1,0:T(1,128)S(1)}, f32[1,128]{1,0:T(1,128)S(1)}, u32[]{:S(2)}, u32[]{:S(2)}) collective-permute-start(f32[1,128]{1,0:T(1,128)S(1)} %get-tuple-element.21), channel_id=1, source_target_pairs={{0,2},{1,3},{2,0},{3,1},{4,6},{5,7},{6,4},{7,5},{8,10},{9,11},{10,... | collective-permute-start | bytes 1544 | tf_op jit(solution)/shard_map/ppermute | solution.py:59
  52.0 1.0 %collective-permute-start.7 = (f32[1,128]{1,0:T(1,128)S(1)}, f32[1,128]{1,0:T(1,128)S(1)}, u32[]{:S(2)}, u32[]{:S(2)}) collective-permute-start(f32[1,128]{1,0:T(1,128)S(1)} %get-tuple-element.20), channel_id=1, source_target_pairs={{0,43},{1,40},{2,41},{3,42},{4,47},{5,44},{6,45},{7,46},{8,51},{9,... | collective-permute-start | bytes 1544 | tf_op jit(solution)/shard_map/ppermute | solution.py:59
  53.0 1.3 %collective-permute-done.9 = f32[1,128]{1,0:T(1,128)S(1)} collective-permute-done((f32[1,128]{1,0:T(1,128)S(1)}, f32[1,128]{1,0:T(1,128)S(1)}, u32[]{:S(2)}, u32[]{:S(2)}) %collective-permute-start.9) | collective-permute-done | bytes 544 | tf_op jit(solution)/shard_map/ppermute | solution.py:59
  54.4 0.7 %collective-permute-done.8 = f32[1,128]{1,0:T(1,128)S(1)} collective-permute-done((f32[1,128]{1,0:T(1,128)S(1)}, f32[1,128]{1,0:T(1,128)S(1)}, u32[]{:S(2)}, u32[]{:S(2)}) %collective-permute-start.8) | collective-permute-done | bytes 544 | tf_op jit(solution)/shard_map/ppermute | solution.py:59
  55.1 4.5 %collective-permute-done.7 = f32[1,128]{1,0:T(1,128)S(1)} collective-permute-done((f32[1,128]{1,0:T(1,128)S(1)}, f32[1,128]{1,0:T(1,128)S(1)}, u32[]{:S(2)}, u32[]{:S(2)}) %collective-permute-start.7) | collective-permute-done | bytes 544 | tf_op jit(solution)/shard_map/ppermute | solution.py:59
  59.5 0.5 compare_select_fusion
  (2 shorter events, 0.0 us)
Async XLA Ops:
  0.0 27.9 %collective-permute-start = (f32[128,512]{1,0:T(8,128)}, f32[128,512]{1,0:T(8,128)S(1)}, u32[]{:S(2)}, u32[]{:S(2)}) collective-permute-start(f32[128,512]{1,0:T(8,128)} %refs_0_.1), channel_id=1, source_target_pairs={{0,60},{1,61},{2,62},{3,63},{4,56},{5,57},{6,58},{7,59},{8,4},{9,5... | collective-permute-start | bytes 786440 | tf_op jit(solution)/shard_map/ppermute | solution.py:59
  4.9 23.0 %collective-permute-start.1 = (f32[128,512]{1,0:T(8,128)}, f32[128,512]{1,0:T(8,128)S(1)}, u32[]{:S(2)}, u32[]{:S(2)}) collective-permute-start(f32[128,512]{1,0:T(8,128)} %refs_0_.1), channel_id=1, source_target_pairs={{0,25},{1,26},{2,27},{3,24},{4,29},{5,30},{6,31},{7,28},{8,33},{9,... | collective-permute-start | bytes 786440 | tf_op jit(solution)/shard_map/ppermute | solution.py:59
  12.9 15.0 %collective-permute-start.2 = (f32[128,512]{1,0:T(8,128)}, f32[128,512]{1,0:T(8,128)S(1)}, u32[]{:S(2)}, u32[]{:S(2)}) collective-permute-start(f32[128,512]{1,0:T(8,128)} %refs_0_.1), channel_id=1, source_target_pairs={{0,2},{1,3},{2,0},{3,1},{4,6},{5,7},{6,4},{7,5},{8,10},{9,11},{10,... | collective-permute-start | bytes 786440 | tf_op jit(solution)/shard_map/ppermute | solution.py:59
  13.3 1.0 %copy-start = (f32[128,512]{1,0:T(8,128)S(1)}, f32[128,512]{1,0:T(8,128)}, u32[]{:S(2)}) copy-start(f32[128,512]{1,0:T(8,128)} %refs_0_.1) | copy-start | bytes 786436
  28.6 14.3 %collective-permute-start.3 = (f32[4,128,512]{2,1,0:T(8,128)S(1)}, f32[4,128,512]{2,1,0:T(8,128)S(1)}, u32[]{:S(2)}, u32[]{:S(2)}) collective-permute-start(f32[4,128,512]{2,1,0:T(8,128)S(1)} %get-tuple-element.15.refs_0_), channel_id=1, source_target_pairs={{0,1},{1,2},{2,3},{3,0},{4,5},{5,6},{6,7},{7,4},{8,9},{9,10},{10,1... | collective-permute-start | bytes 3145736 | tf_op jit(solution)/shard_map/ppermute | solution.py:59
  29.7 13.9 %collective-permute-start.4 = (f32[4,128,512]{2,1,0:T(8,128)S(1)}, f32[4,128,512]{2,1,0:T(8,128)S(1)}, u32[]{:S(2)}, u32[]{:S(2)}) collective-permute-start(f32[4,128,512]{2,1,0:T(8,128)S(1)} %get-tuple-element.15.refs_0_), channel_id=1, source_target_pairs={{0,8},{1,9},{2,10},{3,11},{4,12},{5,13},{6,14},{7,15},{8,16},{9,17... | collective-permute-start | bytes 3145736 | tf_op jit(solution)/shard_map/ppermute | solution.py:59
  30.4 12.5 %all-to-all-start.1 = ((f32[16,1,512]{2,1,0:T(1,128)}), f32[16,1,512]{2,1,0:T(1,128)S(1)}, u32[]{:S(2)}, u32[]{:S(2)}) async-start(f32[16,1,512]{2,1,0:T(1,128)} %get-tuple-element.14), calls=%async_computation.1 | async-start | bytes 65536 | tf_op jit(solution)/shard_map/all_to_all | solution.py:165
  45.5 3.7 %collective-permute-start.5 = (f32[4,1,128]{2,1,0:T(1,128)S(1)}, f32[4,1,128]{2,1,0:T(1,128)S(1)}, u32[]{:S(2)}, u32[]{:S(2)}) collective-permute-start(f32[4,1,128]{2,1,0:T(1,128)S(1)} %get-tuple-element.17), channel_id=1, source_target_pairs={{0,3},{1,0},{2,1},{3,2},{4,7},{5,4},{6,5},{7,6},{8,11},{9,8},{10,9... | collective-permute-start | bytes 6152 | tf_op jit(solution)/shard_map/ppermute | solution.py:59
  45.9 3.6 %collective-permute-start.6 = (f32[4,1,128]{2,1,0:T(1,128)S(1)}, f32[4,1,128]{2,1,0:T(1,128)S(1)}, u32[]{:S(2)}, u32[]{:S(2)}) collective-permute-start(f32[4,1,128]{2,1,0:T(1,128)S(1)} %get-tuple-element.18), channel_id=1, source_target_pairs={{0,56},{1,57},{2,58},{3,59},{4,60},{5,61},{6,62},{7,63},{8,0},{9,1... | collective-permute-start | bytes 6152 | tf_op jit(solution)/shard_map/ppermute | solution.py:59
  49.6 4.8 %collective-permute-start.9 = (f32[1,128]{1,0:T(1,128)S(1)}, f32[1,128]{1,0:T(1,128)S(1)}, u32[]{:S(2)}, u32[]{:S(2)}) collective-permute-start(f32[1,128]{1,0:T(1,128)S(1)} %get-tuple-element.22), channel_id=1, source_target_pairs={{0,12},{1,13},{2,14},{3,15},{4,8},{5,9},{6,10},{7,11},{8,20},{9,21... | collective-permute-start | bytes 1544 | tf_op jit(solution)/shard_map/ppermute | solution.py:59
  51.2 3.9 %collective-permute-start.8 = (f32[1,128]{1,0:T(1,128)S(1)}, f32[1,128]{1,0:T(1,128)S(1)}, u32[]{:S(2)}, u32[]{:S(2)}) collective-permute-start(f32[1,128]{1,0:T(1,128)S(1)} %get-tuple-element.21), channel_id=1, source_target_pairs={{0,2},{1,3},{2,0},{3,1},{4,6},{5,7},{6,4},{7,5},{8,10},{9,11},{10,... | collective-permute-start | bytes 1544 | tf_op jit(solution)/shard_map/ppermute | solution.py:59
  52.0 7.5 %collective-permute-start.7 = (f32[1,128]{1,0:T(1,128)S(1)}, f32[1,128]{1,0:T(1,128)S(1)}, u32[]{:S(2)}, u32[]{:S(2)}) collective-permute-start(f32[1,128]{1,0:T(1,128)S(1)} %get-tuple-element.20), channel_id=1, source_target_pairs={{0,43},{1,40},{2,41},{3,42},{4,47},{5,44},{6,45},{7,46},{8,51},{9,... | collective-permute-start | bytes 1544 | tf_op jit(solution)/shard_map/ppermute | solution.py:59

commit v4 on v1

--- a/solution.py
+++ b/solution.py
@@ -59,7 +59,8 @@
     return lax.ppermute(array, ("core", "z", "xh", "y"), pairs)
 
 
-def head_kernel(own_ref, sums_ref):
+def head_kernel(own_ref, copy_ref, sums_ref):
+    copy_ref[...] = own_ref[...]
     sums_ref[...] = jnp.broadcast_to(
         jnp.sum(own_ref[...], axis=0, keepdims=True)[None], sums_ref.shape
     )
@@ -143,14 +144,17 @@
     vmem = pl.BlockSpec(memory_space=pltpu.VMEM)
     small = pltpu.CompilerParams(vmem_limit_bytes=4 * 1024 * 1024)
     first, second = len(FIRST), len(SECOND)
-    arrived = [send(embeddings, step, 1) for step in FIRST[1:]]
-    sums = pl.pallas_call(
+    embeddings, sums = pl.pallas_call(
         head_kernel,
-        out_shape=jax.ShapeDtypeStruct((16, 1, width), jnp.float32),
+        out_shape=(
+            jax.ShapeDtypeStruct((rows, width), jnp.float32),
+            jax.ShapeDtypeStruct((16, 1, width), jnp.float32),
+        ),
         in_specs=[vmem],
-        out_specs=vmem,
+        out_specs=(vmem, vmem),
         compiler_params=small,
     )(embeddings)
+    arrived = [send(embeddings, step, 1) for step in FIRST[1:]]
     sums = lax.all_to_all(sums, ("core", "z"), 0, 0)
     sums, held = pl.pallas_call(
         middle_kernel,

time: 60.3 us -> 61 us (1.012); the launches traced: 60.1 us -> 60.1 us
  no operation moved by 1% of the time
where the time goes in v4:
time: 61 us; the launch traced here: 60.1 us
  starting transfers between devices  23.2 us (38%)
  waiting for transfers between devices  18.6 us (30%)
  blocking collectives  13.6 us (22%)
  Pallas kernels  2.56 us (4%)
  local copies, waits for them, and re-layouts  0.95 us (2%)
  between operations  0.68 us (1%)
    ppermute x10, starting transfers between devices, send(): return lax.ppermute(array, ('core', 'z', 'xh', 'y'), pairs)  19.7 us
    all_to_all x1, blocking collectives, shards(): sums = lax.all_to_all(sums, ('core', 'z'), 0, 0)  13.6 us
    ppermute x10, waiting for transfers between devices, send(): return lax.ppermute(array, ('core', 'z', 'xh', 'y'), pairs)  10.4 us
    all_to_all x1, waiting for transfers between devices, shards(): sums = lax.all_to_all(sums, ('xl', 'xh', 'y'), 0, 0)  8.16 us
    all_to_all x1, starting transfers between devices, shards(): sums = lax.all_to_all(sums, ('xl', 'xh', 'y'), 0, 0)  3.48 us
    pallas_call x1, Pallas kernels, shards(): pl.pallas_call(best_kernel, out_shape=(jax.ShapeDtypeStruct((first, 1, ro...  1.83 us
  transfers between devices with their start and end apart: 11, of which 7 were waited for; matrix products, arithmetic and copies ran while one was open for 0% of the time, Pallas kernels for 0%

profile of v4, /device:TPU:1, one launch (start us, length us, event | category | flops | bytes accessed | tf_op | source)
XLA Modules:
  0.0 60.1 jit_solution(13280714938785918740)
XLA Ops:
  0.0 0.0 copy-start
  0.0 0.9 %copy-done = f32[128,512]{1,0:T(8,128)S(1)} copy-done((f32[128,512]{1,0:T(8,128)S(1)}, f32[128,512]{1,0:T(8,128)}, u32[]{:S(2)}) %copy-start) | copy-done | bytes 262168
  1.0 5.0 %collective-permute-start = (f32[128,512]{1,0:T(8,128)S(1)}, f32[128,512]{1,0:T(8,128)S(1)}, u32[]{:S(2)}, u32[]{:S(2)}) collective-permute-start(f32[128,512]{1,0:T(8,128)S(1)} %get-tuple-element.17.refs_0_), channel_id=1, source_target_pairs={{0,60},{1,61},{2,62},{3,63},{4,56},{5,57},{6,58},{7,59},{8,4},{9,5... | collective-permute-start | bytes 786440 | tf_op jit(solution)/shard_map/ppermute | solution.py:59
  6.0 8.0 %collective-permute-start.1 = (f32[128,512]{1,0:T(8,128)S(1)}, f32[128,512]{1,0:T(8,128)S(1)}, u32[]{:S(2)}, u32[]{:S(2)}) collective-permute-start(f32[128,512]{1,0:T(8,128)S(1)} %get-tuple-element.17.refs_0_), channel_id=1, source_target_pairs={{0,25},{1,26},{2,27},{3,24},{4,29},{5,30},{6,31},{7,28},{8,33},{9,... | collective-permute-start | bytes 786440 | tf_op jit(solution)/shard_map/ppermute | solution.py:59
  14.0 0.4 collective-permute-start.2
  14.4 13.6 %all_to_all.10.sums_ref = f32[16,1,512]{2,1,0:T(1,128)S(1)} all-to-all(f32[16,1,512]{2,1,0:T(1,128)S(1)} %get-tuple-element.16), channel_id=1, replica_groups=mesh['xl'=2,'core'=2,'z'=8,'xh'=2,'y'=4] {'core','z'}, dimensions={0} | all-to-all | bytes 65536 | tf_op jit(solution)/shard_map/all_to_all | solution.py:158
  28.0 0.0 collective-permute-done.refs_1_
  28.0 0.0 collective-permute-done.1.refs_2_
  28.0 0.0 collective-permute-done.2.refs_3_
  28.0 0.7 %shard_map.29 = (f32[16,1,512]{2,1,0:T(1,128)}, f32[4,128,512]{2,1,0:T(8,128)S(1)}) custom-call(f32[16,1,512]{2,1,0:T(1,128)S(1)} %all_to_all.10.sums_ref, f32[128,512]{1,0:T(8,128)S(1)} %get-tuple-element.17.refs_0_, f32[128,512]{1,0:T(8,128)S(1)} %collective-permute-done.refs_1_, f32[128,512]{1,0:T(8,128)S(1)} %collective-permute-done.1.refs_2_, ...), custom_call_target="tpu_custom_call" | custom-call | tf_op jit(solution)/shard_map/pallas_call | solution.py:159
  28.7 1.1 %collective-permute-start.3 = (f32[4,128,512]{2,1,0:T(8,128)S(1)}, f32[4,128,512]{2,1,0:T(8,128)S(1)}, u32[]{:S(2)}, u32[]{:S(2)}) collective-permute-start(f32[4,128,512]{2,1,0:T(8,128)S(1)} %get-tuple-element.19.refs_0_), channel_id=1, source_target_pairs={{0,1},{1,2},{2,3},{3,0},{4,5},{5,6},{6,7},{7,4},{8,9},{9,10},{10,1... | collective-permute-start | bytes 3145736 | tf_op jit(solution)/shard_map/ppermute | solution.py:59
  29.7 0.9 %collective-permute-start.4 = (f32[4,128,512]{2,1,0:T(8,128)S(1)}, f32[4,128,512]{2,1,0:T(8,128)S(1)}, u32[]{:S(2)}, u32[]{:S(2)}) collective-permute-start(f32[4,128,512]{2,1,0:T(8,128)S(1)} %get-tuple-element.19.refs_0_), channel_id=1, source_target_pairs={{0,8},{1,9},{2,10},{3,11},{4,12},{5,13},{6,14},{7,15},{8,16},{9,17... | collective-permute-start | bytes 3145736 | tf_op jit(solution)/shard_map/ppermute | solution.py:59
  30.6 3.5 %all-to-all-start.1 = ((f32[16,1,512]{2,1,0:T(1,128)}), f32[16,1,512]{2,1,0:T(1,128)S(1)}, u32[]{:S(2)}, u32[]{:S(2)}) async-start(f32[16,1,512]{2,1,0:T(1,128)} %get-tuple-element.18), calls=%async_computation.1 | async-start | bytes 65536 | tf_op jit(solution)/shard_map/all_to_all | solution.py:169
  34.8 8.2 %all-to-all-done.1.sums_ref = f32[16,1,512]{2,1,0:T(1,128)S(1)} async-done(((f32[16,1,512]{2,1,0:T(1,128)}), f32[16,1,512]{2,1,0:T(1,128)S(1)}, u32[]{:S(2)}, u32[]{:S(2)}) %all-to-all-start.1) | async-done | bytes 32800 | tf_op jit(solution)/shard_map/all_to_all | solution.py:169
  42.9 0.0 collective-permute-done.3.refs_1_
  42.9 0.7 %collective-permute-done.4.refs_2_ = f32[4,128,512]{2,1,0:T(8,128)S(1)} collective-permute-done((f32[4,128,512]{2,1,0:T(8,128)S(1)}, f32[4,128,512]{2,1,0:T(8,128)S(1)}, u32[]{:S(2)}, u32[]{:S(2)}) %collective-permute-start.4) | collective-permute-done | bytes 1048608 | tf_op jit(solution)/shard_map/ppermute | solution.py:59
  43.7 1.8 %shard_map.30 = (f32[4,1,128]{2,1,0:T(1,128)S(1)}, f32[4,1,128]{2,1,0:T(1,128)S(1)}, f32[4,1,128]{2,1,0:T(1,128)S(1)}) custom-call(s32[1]{0:T(128)} %copy.3.live_ref, f32[16,1,512]{2,1,0:T(1,128)S(1)} %all-to-all-done.1.sums_ref, f32[4,128,512]{2,1,0:T(8,128)S(1)} %get-tuple-element.19.refs_0_, f32[4,128,512]{2,1,0:T(8,128)S(1)} %collective-permute-done.3.refs_1_, ...), custom_call_target="tpu_custom_call" | custom-call | tf_op jit(solution)/shard_map/pallas_call | solution.py:171
  45.5 0.5 collective-permute-start.5
  46.0 0.5 collective-permute-start.6
  46.4 2.8 %collective-permute-done.5.refs_1_ = f32[4,1,128]{2,1,0:T(1,128)S(1)} collective-permute-done((f32[4,1,128]{2,1,0:T(1,128)S(1)}, f32[4,1,128]{2,1,0:T(1,128)S(1)}, u32[]{:S(2)}, u32[]{:S(2)}) %collective-permute-start.5) | collective-permute-done | bytes 2080 | tf_op jit(solution)/shard_map/ppermute | solution.py:59
  49.2 0.4 collective-permute-done.6.refs_2_
  49.6 1.9 %collective-permute-start.9 = (f32[1,128]{1,0:T(1,128)S(1)}, f32[1,128]{1,0:T(1,128)S(1)}, u32[]{:S(2)}, u32[]{:S(2)}) collective-permute-start(f32[1,128]{1,0:T(1,128)S(1)} %get-tuple-element.26), channel_id=1, source_target_pairs={{0,12},{1,13},{2,14},{3,15},{4,8},{5,9},{6,10},{7,11},{8,20},{9,21... | collective-permute-start | bytes 1544 | tf_op jit(solution)/shard_map/ppermute | solution.py:59
  51.5 0.6 collective-permute-start.8
  52.1 1.0 %collective-permute-start.7 = (f32[1,128]{1,0:T(1,128)S(1)}, f32[1,128]{1,0:T(1,128)S(1)}, u32[]{:S(2)}, u32[]{:S(2)}) collective-permute-start(f32[1,128]{1,0:T(1,128)S(1)} %get-tuple-element.24), channel_id=1, source_target_pairs={{0,43},{1,40},{2,41},{3,42},{4,47},{5,44},{6,45},{7,46},{8,51},{9,... | collective-permute-start | bytes 1544 | tf_op jit(solution)/shard_map/ppermute | solution.py:59
  53.1 1.3 %collective-permute-done.9 = f32[1,128]{1,0:T(1,128)S(1)} collective-permute-done((f32[1,128]{1,0:T(1,128)S(1)}, f32[1,128]{1,0:T(1,128)S(1)}, u32[]{:S(2)}, u32[]{:S(2)}) %collective-permute-start.9) | collective-permute-done | bytes 544 | tf_op jit(solution)/shard_map/ppermute | solution.py:59
  54.4 1.0 %collective-permute-done.8 = f32[1,128]{1,0:T(1,128)S(1)} collective-permute-done((f32[1,128]{1,0:T(1,128)S(1)}, f32[1,128]{1,0:T(1,128)S(1)}, u32[]{:S(2)}, u32[]{:S(2)}) %collective-permute-start.8) | collective-permute-done | bytes 544 | tf_op jit(solution)/shard_map/ppermute | solution.py:59
  55.4 4.2 %collective-permute-done.7 = f32[1,128]{1,0:T(1,128)S(1)} collective-permute-done((f32[1,128]{1,0:T(1,128)S(1)}, f32[1,128]{1,0:T(1,128)S(1)}, u32[]{:S(2)}, u32[]{:S(2)}) %collective-permute-start.7) | collective-permute-done | bytes 544 | tf_op jit(solution)/shard_map/ppermute | solution.py:59
  59.6 0.5 compare_select_fusion
  (2 shorter events, 0.0 us)
Async XLA Ops:
  0.0 0.9 %copy-start = (f32[128,512]{1,0:T(8,128)S(1)}, f32[128,512]{1,0:T(8,128)}, u32[]{:S(2)}) copy-start(f32[128,512]{1,0:T(8,128)} %own_ref.1) | copy-start | bytes 786436
  1.0 27.0 %collective-permute-start = (f32[128,512]{1,0:T(8,128)S(1)}, f32[128,512]{1,0:T(8,128)S(1)}, u32[]{:S(2)}, u32[]{:S(2)}) collective-permute-start(f32[128,512]{1,0:T(8,128)S(1)} %get-tuple-element.17.refs_0_), channel_id=1, source_target_pairs={{0,60},{1,61},{2,62},{3,63},{4,56},{5,57},{6,58},{7,59},{8,4},{9,5... | collective-permute-start | bytes 786440 | tf_op jit(solution)/shard_map/ppermute | solution.py:59
  6.0 22.0 %collective-permute-start.1 = (f32[128,512]{1,0:T(8,128)S(1)}, f32[128,512]{1,0:T(8,128)S(1)}, u32[]{:S(2)}, u32[]{:S(2)}) collective-permute-start(f32[128,512]{1,0:T(8,128)S(1)} %get-tuple-element.17.refs_0_), channel_id=1, source_target_pairs={{0,25},{1,26},{2,27},{3,24},{4,29},{5,30},{6,31},{7,28},{8,33},{9,... | collective-permute-start | bytes 786440 | tf_op jit(solution)/shard_map/ppermute | solution.py:59
  14.0 14.0 %collective-permute-start.2 = (f32[128,512]{1,0:T(8,128)S(1)}, f32[128,512]{1,0:T(8,128)S(1)}, u32[]{:S(2)}, u32[]{:S(2)}) collective-permute-start(f32[128,512]{1,0:T(8,128)S(1)} %get-tuple-element.17.refs_0_), channel_id=1, source_target_pairs={{0,2},{1,3},{2,0},{3,1},{4,6},{5,7},{6,4},{7,5},{8,10},{9,11},{10,... | collective-permute-start | bytes 786440 | tf_op jit(solution)/shard_map/ppermute | solution.py:59
  28.7 14.3 %collective-permute-start.3 = (f32[4,128,512]{2,1,0:T(8,128)S(1)}, f32[4,128,512]{2,1,0:T(8,128)S(1)}, u32[]{:S(2)}, u32[]{:S(2)}) collective-permute-start(f32[4,128,512]{2,1,0:T(8,128)S(1)} %get-tuple-element.19.refs_0_), channel_id=1, source_target_pairs={{0,1},{1,2},{2,3},{3,0},{4,5},{5,6},{6,7},{7,4},{8,9},{9,10},{10,1... | collective-permute-start | bytes 3145736 | tf_op jit(solution)/shard_map/ppermute | solution.py:59
  29.7 13.9 %collective-permute-start.4 = (f32[4,128,512]{2,1,0:T(8,128)S(1)}, f32[4,128,512]{2,1,0:T(8,128)S(1)}, u32[]{:S(2)}, u32[]{:S(2)}) collective-permute-start(f32[4,128,512]{2,1,0:T(8,128)S(1)} %get-tuple-element.19.refs_0_), channel_id=1, source_target_pairs={{0,8},{1,9},{2,10},{3,11},{4,12},{5,13},{6,14},{7,15},{8,16},{9,17... | collective-permute-start | bytes 3145736 | tf_op jit(solution)/shard_map/ppermute | solution.py:59
  30.6 12.3 %all-to-all-start.1 = ((f32[16,1,512]{2,1,0:T(1,128)}), f32[16,1,512]{2,1,0:T(1,128)S(1)}, u32[]{:S(2)}, u32[]{:S(2)}) async-start(f32[16,1,512]{2,1,0:T(1,128)} %get-tuple-element.18), calls=%async_computation.1 | async-start | bytes 65536 | tf_op jit(solution)/shard_map/all_to_all | solution.py:169
  45.5 3.7 %collective-permute-start.5 = (f32[4,1,128]{2,1,0:T(1,128)S(1)}, f32[4,1,128]{2,1,0:T(1,128)S(1)}, u32[]{:S(2)}, u32[]{:S(2)}) collective-permute-start(f32[4,1,128]{2,1,0:T(1,128)S(1)} %get-tuple-element.21), channel_id=1, source_target_pairs={{0,3},{1,0},{2,1},{3,2},{4,7},{5,4},{6,5},{7,6},{8,11},{9,8},{10,9... | collective-permute-start | bytes 6152 | tf_op jit(solution)/shard_map/ppermute | solution.py:59
  46.0 3.6 %collective-permute-start.6 = (f32[4,1,128]{2,1,0:T(1,128)S(1)}, f32[4,1,128]{2,1,0:T(1,128)S(1)}, u32[]{:S(2)}, u32[]{:S(2)}) collective-permute-start(f32[4,1,128]{2,1,0:T(1,128)S(1)} %get-tuple-element.22), channel_id=1, source_target_pairs={{0,56},{1,57},{2,58},{3,59},{4,60},{5,61},{6,62},{7,63},{8,0},{9,1... | collective-permute-start | bytes 6152 | tf_op jit(solution)/shard_map/ppermute | solution.py:59
  49.6 4.8 %collective-permute-start.9 = (f32[1,128]{1,0:T(1,128)S(1)}, f32[1,128]{1,0:T(1,128)S(1)}, u32[]{:S(2)}, u32[]{:S(2)}) collective-permute-start(f32[1,128]{1,0:T(1,128)S(1)} %get-tuple-element.26), channel_id=1, source_target_pairs={{0,12},{1,13},{2,14},{3,15},{4,8},{5,9},{6,10},{7,11},{8,20},{9,21... | collective-permute-start | bytes 1544 | tf_op jit(solution)/shard_map/ppermute | solution.py:59
  51.5 3.9 %collective-permute-start.8 = (f32[1,128]{1,0:T(1,128)S(1)}, f32[1,128]{1,0:T(1,128)S(1)}, u32[]{:S(2)}, u32[]{:S(2)}) collective-permute-start(f32[1,128]{1,0:T(1,128)S(1)} %get-tuple-element.25), channel_id=1, source_target_pairs={{0,2},{1,3},{2,0},{3,1},{4,6},{5,7},{6,4},{7,5},{8,10},{9,11},{10,... | collective-permute-start | bytes 1544 | tf_op jit(solution)/shard_map/ppermute | solution.py:59
  52.1 7.5 %collective-permute-start.7 = (f32[1,128]{1,0:T(1,128)S(1)}, f32[1,128]{1,0:T(1,128)S(1)}, u32[]{:S(2)}, u32[]{:S(2)}) collective-permute-start(f32[1,128]{1,0:T(1,128)S(1)} %get-tuple-element.24), channel_id=1, source_target_pairs={{0,43},{1,40},{2,41},{3,42},{4,47},{5,44},{6,45},{7,46},{8,51},{9,... | collective-permute-start | bytes 1544 | tf_op jit(solution)/shard_map/ppermute | solution.py:59
